TPU v7x, 32 devices: a whole 2x2x4 slice. The times are simulated.
32 devices in a mesh: space: 8 (over z, x), kern: 4 (over y, core).
Axes of the slice: x: 2, y: 2, z: 4, core: 2. Of those that a mesh axis runs over, the one named last changes fastest.
Arguments:
- mask: bfloat16 [4096, 4096], P('space'), may hold values from -1 to 1
- kernels: float32 [2, 16, 512, 512], P(None, 'kern', 'space'), may hold values from -4 to 4
- target: int32 [1024, 1024], P('space'), may hold values 0 or 1
Outputs:
- gradient: float32 [4096, 4096], P('space')
- resist: float32 [1024, 1024], P('space')
All inputs are finite; a program needn't handle non-finite values. No bound on the sum of `target` on one device may be relied on, other than what follows from the above.
Results may differ from a plain program's by a relative error of at most 0.0003.
Values sent between devices are 32-bit elements; how exact they have to be, the bound alone decides.
A program may use at most 64 MiB of HBM per device.

v0:
```python
import functools

import jax
import jax.numpy as jnp
import ml_dtypes
import numpy as np
from jax import lax
from jax.experimental import pallas as pl
from jax.experimental.pallas import tpu as pltpu
from jax.sharding import PartitionSpec as P

N = 4096
B = 512
G = 1024


steepness = 8.0
threshold = 1.5
highest = lax.Precision.HIGHEST
block_limit = 1024


def phases(left, right, modulus):
    product = left[:, None] * right[None, :] % modulus
    return product.astype(jnp.float32) * (2.0 * jnp.pi / modulus)


def column_table(pixels, frequency, length):
    angle = phases(pixels, frequency, length)
    return jnp.concatenate([jnp.cos(angle), -jnp.sin(angle)], axis=1)


def row_table(pixels, frequency, length):
    angle = phases(pixels, frequency, length)
    return jnp.concatenate([jnp.cos(angle), -jnp.sin(angle)], axis=1) / length


def grid_table(frequency, points):
    angle = phases(frequency, jnp.arange(points, dtype=jnp.int32), points)
    return jnp.concatenate([jnp.cos(angle), jnp.sin(angle)], axis=1)


def forward_columns(mask, frequency):
    rows = mask.shape[0]
    span = min(block_limit, N)
    count = frequency.shape[0]

    def step(index, running):
        start = index * span
        table = column_table(start + jnp.arange(span, dtype=jnp.int32), frequency, N)
        piece = lax.dynamic_slice_in_dim(mask, start, span, 1).astype(jnp.float32)
        return running + lax.dot_general(table, piece, (((0,), (1,)), ((), ())), precision=highest)

    running = lax.fori_loop(0, N // span, step, jnp.zeros((2 * count, rows), jnp.float32))
    return running.reshape(2, count, rows)


def forward_rows(arrived):
    count = arrived.shape[1]
    flat = arrived.reshape(2 * count, N)
    frequency = jnp.arange(B, dtype=jnp.int32) - B // 2
    span = min(block_limit, N)

    def step(index, running):
        start = index * span
        table = row_table(start + jnp.arange(span, dtype=jnp.int32), frequency, N)
        piece = lax.dynamic_slice_in_dim(flat, start, span, 1)
        return running + jnp.dot(piece, table, precision=highest)

    running = lax.fori_loop(0, N // span, step, jnp.zeros((2 * count, 2 * B), jnp.float32))
    real_part = running[:count, :B] - running[count:, B:]
    imag_part = running[:count, B:] + running[count:, :B]
    return jnp.stack([real_part, imag_part])


def adjoint_rows(sum_re, sum_im):
    count = sum_re.shape[0]
    stacked = jnp.concatenate(
        [jnp.concatenate([sum_re, sum_im], axis=1), jnp.concatenate([sum_im, -sum_re], axis=1)],
        axis=0,
    )
    frequency = jnp.arange(B, dtype=jnp.int32) - B // 2
    span = min(block_limit, N)

    def step(index, output):
        start = index * span
        table = row_table(start + jnp.arange(span, dtype=jnp.int32), frequency, N)
        piece = lax.dot_general(stacked, table, (((1,), (1,)), ((), ())), precision=highest)
        return lax.dynamic_update_slice_in_dim(output, piece, start, 1)

    output = lax.fori_loop(0, N // span, step, jnp.zeros((2 * count, N), jnp.float32))
    return output.reshape(2, count, N)


def add_columns(total, spectrum, frequency):
    span = min(block_limit, N)

    def step(index, running):
        start = index * span
        table = column_table(start + jnp.arange(span, dtype=jnp.int32), frequency, N)
        piece = lax.dot_general(spectrum, table, (((0,), (1,)), ((), ())), precision=highest)
        current = lax.dynamic_slice_in_dim(running, start, span, 1)
        return lax.dynamic_update_slice_in_dim(running, current + piece, start, 1)

    return lax.fori_loop(0, N // span, step, total)


def local(mask, kernels, target):
    rows = mask.shape[0]
    kern_count = lax.axis_size("kern")
    space_count = lax.axis_size("space")
    group = lax.axis_index("kern")
    per_space = B // space_count
    per_group = per_space // kern_count
    frequency = jnp.arange(B, dtype=jnp.int32) - B // 2
    subset = (
        per_space * jnp.arange(space_count, dtype=jnp.int32)[:, None]
        + per_group * group
        + jnp.arange(per_group, dtype=jnp.int32)[None, :]
    )
    columns = forward_columns(mask, subset.reshape(-1) - B // 2)
    arrived = lax.all_to_all(columns, "space", split_axis=1, concat_axis=2, tiled=True)
    spectrum = lax.all_gather(forward_rows(arrived), "kern", axis=1, tiled=True)
    kern_swap = jnp.swapaxes(kernels, 1, 2)
    kernel_count = kern_swap.shape[2]
    spec_re = spectrum[0][:, None, :]
    spec_im = spectrum[1][:, None, :]
    prod_re = kern_swap[0] * spec_re - kern_swap[1] * spec_im
    prod_im = kern_swap[0] * spec_im + kern_swap[1] * spec_re
    grid = grid_table(frequency, G)
    lifted = jnp.dot(
        jnp.stack([prod_re, prod_im]).reshape(2 * per_space * kernel_count, B),
        grid,
        precision=highest,
    )
    lifted = lifted.reshape(2, per_space, kernel_count, 2 * G)
    coarse_re = lifted[0, :, :, :G] - lifted[1, :, :, G:]
    coarse_im = lifted[0, :, :, G:] + lifted[1, :, :, :G]
    coarse = jnp.stack([coarse_re, coarse_im], axis=1)
    gathered = lax.all_to_all(coarse, "space", split_axis=3, concat_axis=0, tiled=True)
    grid_rows = gathered.shape[3]
    image = lax.dot_general(
        gathered.reshape(B, 2 * kernel_count * grid_rows),
        grid,
        (((0,), (0,)), ((), ())),
        precision=highest,
    )
    image = image.reshape(2, kernel_count, grid_rows, 2 * G)
    field_re = image[0, :, :, :G] - image[1, :, :, G:]
    field_im = image[0, :, :, G:] + image[1, :, :, :G]
    partial_light = jnp.sum(field_re * field_re + field_im * field_im, axis=0) / (B * B)
    intensity = lax.psum(partial_light, "kern")
    resist = jax.nn.sigmoid(steepness * (intensity - threshold))
    slope = 2.0 * (resist - target.astype(jnp.float32)) * steepness * resist * (1.0 - resist)
    scale = 2.0 * slope / (B * B)
    grad_re = scale * field_re
    grad_im = scale * field_im
    mixed = jnp.stack(
        [
            jnp.concatenate([grad_re, grad_im], axis=-1),
            jnp.concatenate([grad_im, -grad_re], axis=-1),
        ]
    )
    mixed = mixed.reshape(2 * kernel_count * grid_rows, 2 * G)
    backward = lax.dot_general(grid, mixed, (((1,), (1,)), ((), ())), precision=highest)
    backward = backward.reshape(B, 2, kernel_count, grid_rows)
    returned = lax.all_to_all(backward, "space", split_axis=0, concat_axis=3, tiled=True)
    back_re = returned[:, 0]
    back_im = returned[:, 1]
    mixed_two = jnp.stack(
        [
            jnp.concatenate([back_re, back_im], axis=-1),
            jnp.concatenate([back_im, -back_re], axis=-1),
        ]
    )
    mixed_two = mixed_two.reshape(2 * per_space * kernel_count, 2 * G)
    spectral = lax.dot_general(mixed_two, grid, (((1,), (1,)), ((), ())), precision=highest)
    spectral = spectral.reshape(2, per_space, kernel_count, B)
    sum_re = jnp.sum(kern_swap[0] * spectral[0] + kern_swap[1] * spectral[1], axis=1)
    sum_im = jnp.sum(kern_swap[0] * spectral[1] - kern_swap[1] * spectral[0], axis=1)
    empty = jnp.zeros((rows, N), jnp.float32)
    shares = (
        lax.psum_scatter(sum_re, "kern", scatter_dimension=0, tiled=True),
        lax.psum_scatter(sum_im, "kern", scatter_dimension=0, tiled=True),
    )
    delta = adjoint_rows(shares[0], shares[1])
    landed = lax.all_to_all(delta, "space", split_axis=2, concat_axis=1, tiled=True)
    ordering = (
        per_group * jnp.arange(kern_count, dtype=jnp.int32)[:, None, None]
        + per_space * jnp.arange(space_count, dtype=jnp.int32)[None, :, None]
        + jnp.arange(per_group, dtype=jnp.int32)[None, None, :]
    )
    ordered_freq = ordering.reshape(-1) - B // 2
    piece = lax.all_gather(landed, "kern", axis=1, tiled=True)
    width = piece.shape[1]
    gradient = add_columns(empty, piece.reshape(2 * width, rows), ordered_freq)
    return (gradient, resist)


MESH = pl.DeviceIdType.MESH


def split_constant(values):
    high = values.astype(np.float32).astype(ml_dtypes.bfloat16)
    low = (values - high.astype(np.float64)).astype(ml_dtypes.bfloat16)
    return jnp.asarray(high), jnp.asarray(low)


def pixel_table():
    f = np.arange(B) - B // 2
    angle = (f[:, None] * np.arange(N)) % N * (2 * np.pi / N)
    return jnp.asarray(np.concatenate([np.cos(angle), -np.sin(angle)]).astype(np.float32))


def coarse_tables(S):
    f = np.arange(B) - B // 2
    points = np.arange(G)
    angle = (f[:, None] * points[None, :]) % G * (2 * np.pi / G)
    c, s = np.cos(angle), np.sin(angle)
    Y = G // S
    cc = c.reshape(B, S, Y).transpose(1, 0, 2)
    ss = s.reshape(B, S, Y).transpose(1, 0, 2)
    lift = np.concatenate([np.concatenate([cc, ss], 2), np.concatenate([-ss, cc], 2)], 1)
    forward = np.concatenate([c.T, s.T], 0)
    backward = np.concatenate([c, s], 0)
    return split_constant(lift) + split_constant(forward) + split_constant(backward)


def halves(value):
    high = value.astype(jnp.bfloat16)
    return high, (value - high.astype(jnp.float32)).astype(jnp.bfloat16)


def dot3(ah, al, bh, bl, dims):
    d = functools.partial(lax.dot_general, dimension_numbers=(dims, ((), ())), preferred_element_type=jnp.float32)
    return d(ah, bh) + (d(al, bh) + d(ah, bl))


NN = ((1,), (0,))
NT = ((1,), (1,))


def remote(src, dst, send, recv, space, kern):
    return pltpu.make_async_remote_copy(
        src_ref=src, dst_ref=dst, send_sem=send, recv_sem=recv, device_id=(space, kern), device_id_type=MESH
    )


def crossed(v):
    return 2 * lax.rem(v, 2) + v // 2


def imaging_kernel(
    S, Q, K4,
    part_ref, kern_mine, target_mine, lh_hbm, ll_hbm, fh_hbm, fl_hbm, bh_hbm, bl_hbm,
    out_ref, resist_ref,
    lh, ll, fh, fl, bh, bl, table_sem,
    kern_ref, target_ref, rbuf, specin, specq,
    specall, ph, pw, out1, in1, field, light, lightin, lightall, out2, in2, sums, rsin, acc,
    ps, pr_, ks, kr_, ts, tr, us, ur, gs, gr, cs, cr, zs, zr,
    spec_s, spec_r, s1, r1, ls, lr, as_, ar, s2, r2, rs, rr,
):
    nx, P_, Y = S // Q, B // S, G // S
    g = P_ // Q
    GQ = G // Q
    sp, kq = lax.axis_index("space"), lax.axis_index("kern")
    z, x = sp // nx, lax.rem(sp, nx)
    blk = crossed(kq) * nx + x
    tables = [
        pltpu.make_async_copy(src, dst, table_sem.at[i])
        for i, (src, dst) in enumerate(
            zip((lh_hbm, ll_hbm, fh_hbm, fl_hbm, bh_hbm, bl_hbm), (lh, ll, fh, fl, bh, bl))
        )
    ]
    for t in tables:
        t.start()

    def member(o):
        b = lax.rem(blk + o, S)
        return b, z * nx + lax.rem(b, nx), crossed(b // nx)

    def zpeer(o):
        q = lax.rem(z + o, Q)
        return q, q * nx + x

    barrier = pltpu.get_barrier_semaphore()
    swapped = z != crossed(kq)
    partner = (crossed(kq) * nx + x, crossed(z))

    def greet(o, c):
        pl.semaphore_signal(barrier, inc=1, device_id=(lax.rem(sp + o, S), kq), device_id_type=MESH)
        return c

    lax.fori_loop(1, S, greet, 0)
    for dk in range(1, Q):
        for xx in range(nx):
            pl.semaphore_signal(
                barrier, inc=1, device_id=(z * nx + xx, lax.rem(kq + dk, Q)), device_id_type=MESH
            )

    @pl.when(swapped)
    def _():
        pl.semaphore_signal(barrier, inc=1, device_id=partner, device_id_type=MESH)

    pl.semaphore_wait(barrier, S - 1 + (Q - 1) * nx + jnp.where(swapped, 1, 0))

    def part_copy(d, slot):
        return remote(part_ref.at[lax.rem(d, nx), d // nx], specin.at[slot], ps.at[d], pr_.at[slot], d, kq)

    def part_start(o, c):
        part_copy(lax.rem(sp + o, S), sp).start()
        return c

    lax.fori_loop(1, S, part_start, 0)
    specin[sp] = part_ref[x, z]

    def kern_copy(k):
        return remote(kern_mine.at[:, k], kern_ref.at[:, k], ks.at[k], kr_.at[k], *partner)

    target_copy = remote(target_mine, target_ref, ts, tr, *partner)

    @pl.when(swapped)
    def _():
        for k in range(K4):
            kern_copy(k).start()
        target_copy.start()

    @pl.when(jnp.logical_not(swapped))
    def _():
        kern_ref[...] = kern_mine[...]
        target_ref[...] = target_mine[...]

    def part_wait(o, c):
        d = lax.rem(sp + o, S)
        part_copy(d, d).wait()
        return c

    lax.fori_loop(1, S, part_wait, 0)
    total = specin[0]
    for d in range(1, S):
        total = total + specin[d]
    specq[...] = total

    def spec_copy(o, slot):
        q, s = zpeer(o)
        return remote(specq, specall.at[slot], spec_s.at[q], spec_r.at[slot], s, kq)

    for o in range(1, Q):
        spec_copy(o, z).start()
    specall[z] = total
    for o in range(1, Q):
        spec_copy(o, zpeer(o)[0]).wait()

    spec = specall[...].reshape(P_, 2 * B)
    sr, si = spec[:, :B], spec[:, B:]
    tables[0].wait()
    tables[1].wait()
    pair = K4 // 2

    def copy1(k, b, s, kk, slot):
        return remote(out1.at[k, b], in1.at[k, slot], s1.at[k, b], r1.at[k, slot], s, kk)

    for h in range(2):
        @pl.when(swapped)
        def _():
            for j in range(pair):
                kern_copy(h * pair + j).wait()

        for k in range(h * pair, h * pair + pair):
            kr, ki = kern_ref[0, k], kern_ref[1, k]
            rows = pl.ds(k * P_, P_)
            ph[rows, :B], pw[rows, :B] = halves(kr * sr - ki * si)
            ph[rows, B:], pw[rows, B:] = halves(kr * si + ki * sr)
        rows = pl.ds(h * pair * P_, pair * P_)

        def lift(b):
            return dot3(ph[rows, :], pw[rows, :], lh[b], ll[b], NN).reshape(pair, P_, 2 * Y)

        def step(o, c):
            b, s, kk = member(o)
            value = lift(b)
            for j in range(pair):
                out1[h * pair + j, b] = value[j]
            for j in range(pair):
                copy1(h * pair + j, b, s, kk, blk).start()
            return c

        lax.fori_loop(1, S, step, 0)
        value = lift(blk)
        for j in range(pair):
            in1[h * pair + j, blk] = value[j]

    for t in tables[2:]:
        t.wait()
    chunk = 256

    def image(k, c):
        def arrive(o, c):
            b, s, kk = member(o)
            copy1(k, b, s, kk, b).wait_recv()
            return c

        lax.fori_loop(1, S, arrive, 0)
        dh, dl = halves(in1[k].reshape(B, 2 * Y))

        def part(j, c):
            rows = pl.ds(pl.multiple_of(j * chunk, chunk), chunk)
            low = pl.ds(pl.multiple_of(G + j * chunk, chunk), chunk)
            a = dot3(fh[rows, :], fl[rows, :], dh, dl, NN)
            b = dot3(fh[low, :], fl[low, :], dh, dl, NN)
            re = a[:, :Y] - b[:, Y:]
            im = a[:, Y:] + b[:, :Y]
            field[k, rows, :Y] = re
            field[k, rows, Y:] = im
            power = re * re + im * im

            @pl.when(k == 0)
            def _():
                light[rows, :] = power

            @pl.when(k > 0)
            def _():
                light[rows, :] = light[rows, :] + power

            return c

        return lax.fori_loop(0, G // chunk, part, c)

    lax.fori_loop(0, K4, image, 0)

    quarter = lambda q: pl.ds(pl.multiple_of(q * GQ, GQ), GQ)

    def light_copy(o, slot):
        q, s = zpeer(o)
        return remote(light.at[quarter(q)], lightin.at[slot], ls.at[q], lr.at[slot], s, kq)

    for o in range(1, Q):
        light_copy(o, z).start()
    lightin[z] = light[quarter(z), :]
    for o in range(1, Q):
        light_copy(o, zpeer(o)[0]).wait()
    total = lightin[0]
    for q in range(1, Q):
        total = total + lightin[q]
    lightall[z] = total * (1.0 / (B * B))

    def all_copy(o, slot):
        q, s = zpeer(o)
        return remote(lightall.at[z], lightall.at[slot], as_.at[q], ar.at[slot], s, kq)

    for o in range(1, Q):
        all_copy(o, z).start()
    for o in range(1, Q):
        all_copy(o, zpeer(o)[0]).wait_recv()

    @pl.when(swapped)
    def _():
        target_copy.wait()

    for q in range(Q):
        rows = pl.ds(q * GQ, GQ)
        resist = jax.nn.sigmoid(steepness * (lightall[q] - threshold))
        rbuf[rows, :] = resist
        light[rows, :] = (4.0 * steepness / (B * B)) * (resist - target_ref[rows, :]) * resist * (1.0 - resist)

    resist_copy = remote(rbuf, resist_ref, us, ur, *partner)

    @pl.when(swapped)
    def _():
        resist_copy.start()

    @pl.when(jnp.logical_not(swapped))
    def _():
        resist_ref[...] = rbuf[...]

    def copy2(k, b, s, kk, slot):
        return remote(out2.at[k, b], in2.at[k, slot], s2.at[k, b], r2.at[k, slot], s, kk)

    def back(k, c):
        scale = light[...]
        scale = jnp.concatenate([scale, scale], axis=1)
        dh, dl = halves(field[k] * scale)

        def part(j, c):
            rows = pl.ds(pl.multiple_of(j * chunk, chunk), chunk)
            low = pl.ds(pl.multiple_of(B + j * chunk, chunk), chunk)
            a = dot3(bh[rows, :], bl[rows, :], dh, dl, NN)
            b = dot3(bh[low, :], bl[low, :], dh, dl, NN)
            value = jnp.concatenate([a[:, :Y] + b[:, Y:], a[:, Y:] - b[:, :Y]], axis=1)
            out2[k, pl.ds(j * (chunk // P_), chunk // P_)] = value.reshape(chunk // P_, P_, 2 * Y)
            return c

        lax.fori_loop(0, B // chunk, part, c)

        def launch(o, c):
            b, s, kk = member(o)
            copy2(k, b, s, kk, blk).start()
            return c

        lax.fori_loop(1, S, launch, 0)
        in2[k, blk] = out2[k, blk]
        return c

    lax.fori_loop(0, K4, back, 0)

    sum_re = jnp.zeros((P_, B), jnp.float32)
    sum_im = jnp.zeros((P_, B), jnp.float32)
    for h in range(2):
        for j in range(pair):
            def arrive2(o, c):
                b, s, kk = member(o)
                copy2(h * pair + j, b, s, kk, b).wait_recv()
                return c

            lax.fori_loop(1, S, arrive2, 0)
        acc[...] = jnp.zeros_like(acc)

        def add(s, c):
            dh, dl = halves(in2[pl.ds(h * pair, pair), s].reshape(pair * P_, 2 * Y))
            acc[...] += dot3(dh, dl, lh[s], ll[s], NT)
            return c

        lax.fori_loop(0, S, add, 0)
        for j in range(pair):
            k = h * pair + j
            kr, ki = kern_ref[0, k], kern_ref[1, k]
            pr, pi = acc[pl.ds(j * P_, P_), :B], acc[pl.ds(j * P_, P_), B:]
            sum_re = sum_re + kr * pr + ki * pi
            sum_im = sum_im + kr * pi - ki * pr
    sums[:, :, :B] = sum_re.reshape(Q, g, B)
    sums[:, :, B:] = sum_im.reshape(Q, g, B)

    def sum_copy(o, slot):
        q, s = zpeer(o)
        return remote(sums.at[q], rsin.at[slot], rs.at[q], rr.at[slot], s, kq)

    for o in range(1, Q):
        sum_copy(o, z).start()
    rsin[z] = sums[z]
    for o in range(1, Q):
        sum_copy(o, zpeer(o)[0]).wait()
    total = rsin[0]
    for q in range(1, Q):
        total = total + rsin[q]
    out_ref[blk, z] = total

    def z_copy(o, slot):
        q, s = zpeer(o)
        return remote(out_ref.at[blk, z], out_ref.at[blk, slot], zs.at[q], zr.at[slot], s, kq)

    def z_from(o):
        q, s = zpeer(o)
        return remote(out_ref.at[blk, q], out_ref.at[blk, q], zs.at[q], zr.at[q], s, kq)

    for o in range(1, Q):
        z_copy(o, z).start()
    for o in range(1, Q):
        z_from(o).wait_recv()
    kc = kq + 1 - 2 * lax.rem(kq, 2)
    others = []
    for dx in range(nx):
        for dy in range(2):
            if dx or dy:
                kk, xx = lax.rem(kq + 2 * dy, Q), lax.rem(x + dx, nx)
                xf = lax.rem(x + nx - dx, nx)
                others.append((kk, xx, crossed(kk) * nx + xx, xf, crossed(kk) * nx + xf))

    def to_core(b):
        return remote(out_ref.at[b], out_ref.at[b], cs.at[b], cr.at[b], sp, kc)

    def to_brick(other):
        kk, xx, b, xf, bf = other
        return remote(out_ref.at[blk], out_ref.at[blk], gs.at[b], gr.at[blk], z * nx + xx, kk)

    def from_brick(other):
        kk, xx, b, xf, bf = other
        return remote(out_ref.at[bf], out_ref.at[bf], gs.at[b], gr.at[bf], z * nx + xf, kk)

    for other in others:
        to_brick(other).start()
    to_core(blk).start()
    for other in others:
        from_brick(other).wait_recv()
        to_core(other[4]).start()
    for kk, xx in [(kq, x)] + [(o[0], o[3]) for o in others]:
        mine = crossed(kk) * nx + xx
        theirs = crossed(kk + 1 - 2 * lax.rem(kk, 2)) * nx + xx
        to_core(mine).wait_send()
        to_core(theirs).wait_recv()
    for other in others:
        to_brick(other).wait_send()
    for o in range(1, Q):
        z_copy(o, z).wait_send()

    @pl.when(swapped)
    def _():
        resist_copy.wait()

    for o in range(1, Q):
        all_copy(o, z).wait_send()

    def drain(k, c):
        def one(o, c):
            b, s, kk = member(o)
            copy1(k, b, s, kk, blk).wait_send()
            copy2(k, b, s, kk, blk).wait_send()
            return c

        return lax.fori_loop(1, S, one, c)

    lax.fori_loop(0, K4, drain, 0)


def call(kernel, outs, specs, scratch, cid, args, mib):
    vm = pl.BlockSpec(memory_space=pltpu.VMEM)
    return pl.pallas_call(
        kernel,
        out_shape=outs,
        in_specs=specs,
        out_specs=jax.tree.map(lambda _: vm, outs),
        scratch_shapes=scratch,
        compiler_params=pltpu.CompilerParams(
            collective_id=cid, has_side_effects=True, vmem_limit_bytes=mib * 2**20
        ),
    )(*args)


def fast(S, Q, mask, kernels, target):
    f32, bf16 = jnp.float32, jnp.bfloat16
    nx, P_, Y, R = S // Q, B // S, G // S, N // S
    g, K4 = P_ // Q, kernels.shape[1]
    DMA = pltpu.SemaphoreType.DMA
    vm, any_ = pl.BlockSpec(memory_space=pltpu.VMEM), pl.BlockSpec(memory_space=pl.ANY)
    high = lax.Precision.HIGH
    sp, kq = lax.axis_index("space"), lax.axis_index("kern")
    table = pixel_table()
    C = B // Q

    rows = jnp.concatenate([lax.dynamic_slice_in_dim(table, part * B + crossed(kq) * C, C, 0) for part in range(2)], axis=0)
    columns = lax.dot_general(rows, mask.astype(f32), (((1,), (1,)), ((), ())), precision=high)
    slab = lax.dynamic_slice_in_dim(table, sp * R, R, 1) * (1.0 / N)
    t = lax.dot_general(columns, slab, (((1,), (1,)), ((), ())), precision=high)
    part = jnp.concatenate([t[:C, :B] - t[C:, B:], t[:C, B:] + t[C:, :B]], axis=1)

    consts = coarse_tables(S)
    V = pltpu.VMEM
    total, resist = call(
        functools.partial(imaging_kernel, S, Q, K4),
        (jax.ShapeDtypeStruct((S, Q, g, 2 * B), f32), jax.ShapeDtypeStruct((G, Y), f32)),
        [vm, vm, vm] + [any_] * 6,
        [V(c.shape, bf16) for c in consts] + [DMA((6,))] + [
            V((2, K4, P_, B), f32), V((G, Y), f32), V((G, Y), f32),
            V((S, g, 2 * B), f32), V((g, 2 * B), f32),
            V((Q, g, 2 * B), f32),
            V((K4 * P_, 2 * B), bf16), V((K4 * P_, 2 * B), bf16),
            V((K4, S, P_, 2 * Y), f32), V((K4, S, P_, 2 * Y), f32),
            V((K4, G, 2 * Y), f32), V((G, Y), f32),
            V((Q, G // Q, Y), f32), V((Q, G // Q, Y), f32),
            V((K4, S, P_, 2 * Y), f32), V((K4, S, P_, 2 * Y), f32),
            V((Q, g, 2 * B), f32), V((Q, g, 2 * B), f32),
            V((K4 // 2 * P_, 2 * B), f32),
            DMA((S,)), DMA((S,)), DMA((K4,)), DMA((K4,)), DMA, DMA, DMA, DMA,
            DMA((S,)), DMA((S,)), DMA((S,)), DMA((S,)), DMA((Q,)), DMA((Q,)),
            DMA((Q,)), DMA((Q,)), DMA((K4, S)), DMA((K4, S)),
            DMA((Q,)), DMA((Q,)), DMA((Q,)), DMA((Q,)),
            DMA((K4, S)), DMA((K4, S)), DMA((Q,)), DMA((Q,)),
        ],
        1, (part.reshape(nx, Q, g, 2 * B), kernels, target.T.astype(f32)) + consts, 58,
    )

    total = total.reshape(B, 2 * B)
    a, b = slab[:B], slab[B:]
    delta = jnp.concatenate([
        jnp.dot(total, slab, precision=high),
        jnp.dot(total, jnp.concatenate([-b, a], axis=0), precision=high),
    ], axis=0)
    gradient = lax.dot_general(lax.optimization_barrier(delta), table, (((0,), (0,)), ((), ())), precision=high)
    return gradient, resist.T


def solution(mesh):
    in_specs = (P("space", None), P(None, "kern", "space", None), P("space", None))
    out_specs = (P("space", None), P("space", None))
    S, Q = mesh.shape["space"], mesh.shape["kern"]
    whole_tiles = Q == 4 and S % Q == 0 and (B // S // Q) % 16 == 0 and (G // S) % 128 == 0
    body = functools.partial(fast, S, Q) if whole_tiles else local
    return jax.shard_map(body, mesh=mesh, in_specs=in_specs, out_specs=out_specs, check_vma=False)
```

profile of v0, /device:TPU:1, one launch (start us, length us, event | category | flops | bytes accessed | tf_op | source)
XLA Modules:
  0.0 231.5 jit_solution(1767275368692424936)
XLA Ops:
  0.7 1.2 copy.12
  1.9 0.8 convert_bitcast_fusion.target_mine
  2.7 1.8 dynamic-slice_multiply_fusion
  4.6 0.2 slice_negate_fusion
  4.8 0.0 copy-start.1
  4.8 2.7 %constant_dynamic-slice_fusion.1 = (f32[128,4096]{1,0:T(8,128)S(1)}, f32[128,4096]{1,0:T(8,128)S(1)}) fusion(f32[1024,4096]{1,0:T(8,128)} %constant.53.clone, s32[]{:T(128)S(6)} %select_n.16, s32[]{:T(128)S(6)} %select_n.17), kind=kLoop, calls=%fused_computation.22 | loop fusion | bytes 8388616 | tf_op jit(solution)/shard_map/dynamic_slice | solution.py:639
  7.5 0.8 copy-done.1
  8.2 2.4 %fusion = f32[256,512]{1,0:T(8,128)S(1)} fusion(bf16[512,4096]{1,0:T(8,128)(2,1)S(1)} %copy-done.1, f32[128,4096]{1,0:T(8,128)S(1)} %get-tuple-element.9, f32[128,4096]{1,0:T(8,128)S(1)} %get-tuple-element.8), kind=kOutput, calls=%fused_computation | convolution fusion | flops 3222274048 | bytes 8912896 | tf_op jit(solution)/shard_map/dot_general | solution.py:640
  10.6 2.7 %fusion.9 = f32[256,1024]{1,0:T(8,128)S(1)} fusion(f32[256,512]{1,0:T(8,128)S(1)} %fusion, f32[1024,4096]{1,0:T(8,128)} %constant.53.clone, s32[]{:T(128)S(6)} %select_n.18), kind=kOutput, calls=%fused_computation.11 | convolution fusion | flops 805830656 | bytes 3670020 | tf_op jit(solution)/shard_map/dot_general | solution.py:642
  13.3 0.1 slice_subtract_fusion
  13.4 0.8 pad_maximum_fusion.1
  14.2 188.5 %shard_map.113 = (f32[8,4,16,1024]{3,2,1,0:T(8,128)}, f32[1024,128]{1,0:T(8,128)}) custom-call(f32[2,4,16,1024]{3,2,1,0:T(8,128)} %bitcast.13, f32[2,4,64,512]{3,2,1,0:T(8,128)} %kern_mine.1, f32[1024,128]{1,0:T(8,128)} %convert_bitcast_fusion.target_mine, bf16[8,1024,256]{2,1,0:T(8,128)(2,1)} %constant.54.clone.lh_hbm, ...), custom_call_target="tpu_custom_call" | custom-call | tf_op jit(solution)/shard_map/pallas_call | solution.py:616
  202.7 0.0 copy-start
  202.7 3.6 %fusion.4 = f32[512,512]{1,0:T(8,128)S(1)} fusion(f32[512,1024]{1,0:T(8,128)} %bitcast.11, f32[512,512]{1,0:T(8,128)S(1)} %get-tuple-element.11, f32[512,512]{1,0:T(8,128)S(1)} %get-tuple-element.10), kind=kOutput, calls=%fused_computation.4 | convolution fusion | flops 1611137024 | bytes 5242880 | tf_op jit(solution)/shard_map/dot_general | solution.py:675
  206.3 0.0 copy-done
  206.3 3.5 %fusion.8 = f32[512,512]{1,0:T(8,128)S(1)} fusion(f32[512,1024]{1,0:T(8,128)S(1)} %bitcast.12, f32[1024,4096]{1,0:T(8,128)} %constant.53.clone, s32[]{:T(128)S(6)} %select_n.18), kind=kOutput, calls=%fused_computation.10 | convolution fusion | flops 1611137024 | bytes 5242884 | tf_op jit(solution)/shard_map/dot_general | solution.py:674
  209.9 0.0 copy-start.2
  209.9 0.2 pad_maximum_fusion
  210.1 0.9 copy-done.2
  210.9 1.0 copy.13
  211.9 19.6 %fusion.18 = f32[512,4096]{1,0:T(8,128)} fusion(f32[1024,512]{1,0:T(8,128)S(1)} %pad_maximum_fusion, f32[1024,4096]{1,0:T(8,128)} %constant.53.clone), kind=kOutput, calls=%fused_computation.27 | convolution fusion | flops 12884901888 | bytes 27262976 | tf_op jit(solution)/shard_map/dot_general | solution.py:677
Async XLA Ops:
  4.8 3.5 %copy-start.1 = (bf16[512,4096]{1,0:T(8,128)(2,1)S(1)}, bf16[512,4096]{1,0:T(8,128)(2,1)}, u32[]{:S(2)}) copy-start(bf16[512,4096]{1,0:T(8,128)(2,1)} %param.10) | copy-start | bytes 12582916
  202.7 3.6 %copy-start = (f32[8,4,16,1024]{3,2,1,0:T(8,128)S(1)}, f32[8,4,16,1024]{3,2,1,0:T(8,128)}, u32[]{:S(2)}) copy-start(f32[8,4,16,1024]{3,2,1,0:T(8,128)} %get-tuple-element.4) | copy-start | bytes 6291460
  209.9 1.0 copy-start.2
where the time goes:
time: 232 us
  Pallas kernels  188 us (81%)
  matrix products  31.8 us (14%)
  local copies, waits for them, and re-layouts  6.52 us (3%)
  other arithmetic  3.94 us (2%)
    pallas_call x1, Pallas kernels, call(): pl.pallas_call(kernel, out_shape=outs, in_specs=specs, out_specs=jax.tree...  188 us
    dot_general x1, matrix products, fast(): lax.dot_general(lax.optimization_barrier(delta), table, (((0,), (0,)), ((...  19.6 us

commit v1 on v0

v1 whole, which is shorter than its diff:
```python
import functools

import jax
import jax.numpy as jnp
import ml_dtypes
import numpy as np
from jax import lax
from jax.experimental import pallas as pl
from jax.experimental.pallas import tpu as pltpu
from jax.sharding import PartitionSpec as P

N = 4096
B = 512
G = 1024


steepness = 8.0
threshold = 1.5
highest = lax.Precision.HIGHEST
block_limit = 1024


def phases(left, right, modulus):
    product = left[:, None] * right[None, :] % modulus
    return product.astype(jnp.float32) * (2.0 * jnp.pi / modulus)


def column_table(pixels, frequency, length):
    angle = phases(pixels, frequency, length)
    return jnp.concatenate([jnp.cos(angle), -jnp.sin(angle)], axis=1)


def row_table(pixels, frequency, length):
    angle = phases(pixels, frequency, length)
    return jnp.concatenate([jnp.cos(angle), -jnp.sin(angle)], axis=1) / length


def grid_table(frequency, points):
    angle = phases(frequency, jnp.arange(points, dtype=jnp.int32), points)
    return jnp.concatenate([jnp.cos(angle), jnp.sin(angle)], axis=1)


def forward_columns(mask, frequency):
    rows = mask.shape[0]
    span = min(block_limit, N)
    count = frequency.shape[0]

    def step(index, running):
        start = index * span
        table = column_table(start + jnp.arange(span, dtype=jnp.int32), frequency, N)
        piece = lax.dynamic_slice_in_dim(mask, start, span, 1).astype(jnp.float32)
        return running + lax.dot_general(table, piece, (((0,), (1,)), ((), ())), precision=highest)

    running = lax.fori_loop(0, N // span, step, jnp.zeros((2 * count, rows), jnp.float32))
    return running.reshape(2, count, rows)


def forward_rows(arrived):
    count = arrived.shape[1]
    flat = arrived.reshape(2 * count, N)
    frequency = jnp.arange(B, dtype=jnp.int32) - B // 2
    span = min(block_limit, N)

    def step(index, running):
        start = index * span
        table = row_table(start + jnp.arange(span, dtype=jnp.int32), frequency, N)
        piece = lax.dynamic_slice_in_dim(flat, start, span, 1)
        return running + jnp.dot(piece, table, precision=highest)

    running = lax.fori_loop(0, N // span, step, jnp.zeros((2 * count, 2 * B), jnp.float32))
    real_part = running[:count, :B] - running[count:, B:]
    imag_part = running[:count, B:] + running[count:, :B]
    return jnp.stack([real_part, imag_part])


def adjoint_rows(sum_re, sum_im):
    count = sum_re.shape[0]
    stacked = jnp.concatenate(
        [jnp.concatenate([sum_re, sum_im], axis=1), jnp.concatenate([sum_im, -sum_re], axis=1)],
        axis=0,
    )
    frequency = jnp.arange(B, dtype=jnp.int32) - B // 2
    span = min(block_limit, N)

    def step(index, output):
        start = index * span
        table = row_table(start + jnp.arange(span, dtype=jnp.int32), frequency, N)
        piece = lax.dot_general(stacked, table, (((1,), (1,)), ((), ())), precision=highest)
        return lax.dynamic_update_slice_in_dim(output, piece, start, 1)

    output = lax.fori_loop(0, N // span, step, jnp.zeros((2 * count, N), jnp.float32))
    return output.reshape(2, count, N)


def add_columns(total, spectrum, frequency):
    span = min(block_limit, N)

    def step(index, running):
        start = index * span
        table = column_table(start + jnp.arange(span, dtype=jnp.int32), frequency, N)
        piece = lax.dot_general(spectrum, table, (((0,), (1,)), ((), ())), precision=highest)
        current = lax.dynamic_slice_in_dim(running, start, span, 1)
        return lax.dynamic_update_slice_in_dim(running, current + piece, start, 1)

    return lax.fori_loop(0, N // span, step, total)


def local(mask, kernels, target):
    rows = mask.shape[0]
    kern_count = lax.axis_size("kern")
    space_count = lax.axis_size("space")
    group = lax.axis_index("kern")
    per_space = B // space_count
    per_group = per_space // kern_count
    frequency = jnp.arange(B, dtype=jnp.int32) - B // 2
    subset = (
        per_space * jnp.arange(space_count, dtype=jnp.int32)[:, None]
        + per_group * group
        + jnp.arange(per_group, dtype=jnp.int32)[None, :]
    )
    columns = forward_columns(mask, subset.reshape(-1) - B // 2)
    arrived = lax.all_to_all(columns, "space", split_axis=1, concat_axis=2, tiled=True)
    spectrum = lax.all_gather(forward_rows(arrived), "kern", axis=1, tiled=True)
    kern_swap = jnp.swapaxes(kernels, 1, 2)
    kernel_count = kern_swap.shape[2]
    spec_re = spectrum[0][:, None, :]
    spec_im = spectrum[1][:, None, :]
    prod_re = kern_swap[0] * spec_re - kern_swap[1] * spec_im
    prod_im = kern_swap[0] * spec_im + kern_swap[1] * spec_re
    grid = grid_table(frequency, G)
    lifted = jnp.dot(
        jnp.stack([prod_re, prod_im]).reshape(2 * per_space * kernel_count, B),
        grid,
        precision=highest,
    )
    lifted = lifted.reshape(2, per_space, kernel_count, 2 * G)
    coarse_re = lifted[0, :, :, :G] - lifted[1, :, :, G:]
    coarse_im = lifted[0, :, :, G:] + lifted[1, :, :, :G]
    coarse = jnp.stack([coarse_re, coarse_im], axis=1)
    gathered = lax.all_to_all(coarse, "space", split_axis=3, concat_axis=0, tiled=True)
    grid_rows = gathered.shape[3]
    image = lax.dot_general(
        gathered.reshape(B, 2 * kernel_count * grid_rows),
        grid,
        (((0,), (0,)), ((), ())),
        precision=highest,
    )
    image = image.reshape(2, kernel_count, grid_rows, 2 * G)
    field_re = image[0, :, :, :G] - image[1, :, :, G:]
    field_im = image[0, :, :, G:] + image[1, :, :, :G]
    partial_light = jnp.sum(field_re * field_re + field_im * field_im, axis=0) / (B * B)
    intensity = lax.psum(partial_light, "kern")
    resist = jax.nn.sigmoid(steepness * (intensity - threshold))
    slope = 2.0 * (resist - target.astype(jnp.float32)) * steepness * resist * (1.0 - resist)
    scale = 2.0 * slope / (B * B)
    grad_re = scale * field_re
    grad_im = scale * field_im
    mixed = jnp.stack(
        [
            jnp.concatenate([grad_re, grad_im], axis=-1),
            jnp.concatenate([grad_im, -grad_re], axis=-1),
        ]
    )
    mixed = mixed.reshape(2 * kernel_count * grid_rows, 2 * G)
    backward = lax.dot_general(grid, mixed, (((1,), (1,)), ((), ())), precision=highest)
    backward = backward.reshape(B, 2, kernel_count, grid_rows)
    returned = lax.all_to_all(backward, "space", split_axis=0, concat_axis=3, tiled=True)
    back_re = returned[:, 0]
    back_im = returned[:, 1]
    mixed_two = jnp.stack(
        [
            jnp.concatenate([back_re, back_im], axis=-1),
            jnp.concatenate([back_im, -back_re], axis=-1),
        ]
    )
    mixed_two = mixed_two.reshape(2 * per_space * kernel_count, 2 * G)
    spectral = lax.dot_general(mixed_two, grid, (((1,), (1,)), ((), ())), precision=highest)
    spectral = spectral.reshape(2, per_space, kernel_count, B)
    sum_re = jnp.sum(kern_swap[0] * spectral[0] + kern_swap[1] * spectral[1], axis=1)
    sum_im = jnp.sum(kern_swap[0] * spectral[1] - kern_swap[1] * spectral[0], axis=1)
    empty = jnp.zeros((rows, N), jnp.float32)
    shares = (
        lax.psum_scatter(sum_re, "kern", scatter_dimension=0, tiled=True),
        lax.psum_scatter(sum_im, "kern", scatter_dimension=0, tiled=True),
    )
    delta = adjoint_rows(shares[0], shares[1])
    landed = lax.all_to_all(delta, "space", split_axis=2, concat_axis=1, tiled=True)
    ordering = (
        per_group * jnp.arange(kern_count, dtype=jnp.int32)[:, None, None]
        + per_space * jnp.arange(space_count, dtype=jnp.int32)[None, :, None]
        + jnp.arange(per_group, dtype=jnp.int32)[None, None, :]
    )
    ordered_freq = ordering.reshape(-1) - B // 2
    piece = lax.all_gather(landed, "kern", axis=1, tiled=True)
    width = piece.shape[1]
    gradient = add_columns(empty, piece.reshape(2 * width, rows), ordered_freq)
    return (gradient, resist)


MESH = pl.DeviceIdType.MESH


def split_constant(values):
    high = values.astype(np.float32).astype(ml_dtypes.bfloat16)
    low = (values - high.astype(np.float64)).astype(ml_dtypes.bfloat16)
    return jnp.asarray(high), jnp.asarray(low)


def pixel_table():
    f = np.arange(B) - B // 2
    angle = (f[:, None] * np.arange(N)) % N * (2 * np.pi / N)
    return jnp.asarray(np.concatenate([np.cos(angle), -np.sin(angle)]).astype(np.float32))


def coarse_tables():
    f = np.arange(B) - B // 2
    points = np.arange(G)
    angle = (f[:, None] * points[None, :]) % G * (2 * np.pi / G)
    c, s = np.cos(angle), np.sin(angle)
    order = np.arange(G).reshape(8, 2, 2, G // 32).transpose(1, 2, 0, 3).reshape(2, G // 2)
    lift = np.stack([np.block([[c.T[o], -s.T[o]], [s.T[o], c.T[o]]]) for o in order])
    W = G // PARTS
    image = np.stack([np.concatenate([c[:, j * W : j * W + W], s[:, j * W : j * W + W]], 1) for j in range(PARTS)])
    return split_constant(lift) + split_constant(image)


def halves(value):
    high = value.astype(jnp.bfloat16)
    return high, (value - high.astype(jnp.float32)).astype(jnp.bfloat16)


def dot3(ah, al, bh, bl, dims):
    d = functools.partial(lax.dot_general, dimension_numbers=(dims, ((), ())), preferred_element_type=jnp.float32)
    return d(ah, bh) + (d(al, bh) + d(ah, bl))


NN = ((1,), (0,))
NT = ((1,), (1,))
PARTS = 4
DIMS = "yhlx"
ORDERS = ("xylh", "ylxh", "lxyh", "yxlh")
SPACE_ORDERS = ("xlh", "lxh", "xlh", "lxh")


def remote(src, dst, send, recv, device):
    return pltpu.make_async_remote_copy(
        src_ref=src, dst_ref=dst, send_sem=send, recv_sem=recv, device_id=device, device_id_type=MESH
    )


def crossed(v):
    return 2 * lax.rem(v, 2) + v // 2


def index(dims, fixed, lanes):
    return tuple(fixed.get(d, slice(None)) for d in dims) + (slice(None), lanes)


def without(dims, gone):
    return "".join(d for d in dims if d not in gone)


class Scatter:
    def __init__(self, me, partner, src, bufs, dims, order, lanes, send, recv):
        self.me, self.partner, self.refs, self.dims = me, partner, [src] + list(bufs), dims
        self.order, self.lanes, self.send, self.recv = order, lanes, send, recv

    def copy(self, t):
        d = self.order[t]
        left = without(self.dims, self.order[:t])
        return remote(
            self.refs[t].at[index(left, {d: 1 - self.me[d]}, self.lanes)],
            self.refs[t + 1].at[index(without(left, d), {}, self.lanes)],
            self.send.at[t], self.recv.at[t], self.partner[d],
        )

    def start(self, t):
        self.copy(t).start()

    def finish(self, t):
        self.copy(t).wait_recv()
        d = self.order[t]
        left = without(self.dims, self.order[:t])
        own = self.refs[t][index(left, {d: self.me[d]}, self.lanes)]
        there = index(without(left, d), {}, self.lanes)
        self.refs[t + 1][there] = self.refs[t + 1][there] + own

    def drain(self):
        for t in range(len(self.order)):
            self.copy(t).wait_send()


class Gather:
    def __init__(self, me, partner, ref, dims, order, lanes, send, recv):
        self.me, self.partner, self.ref, self.dims = me, partner, ref, dims
        self.order, self.lanes, self.send, self.recv = order, lanes, send, recv

    def copy(self, t, theirs):
        fixed = {d: self.me[d] for d in self.order[t:]}
        if theirs:
            fixed[self.order[t]] = 1 - fixed[self.order[t]]
        view = self.ref.at[index(self.dims, fixed, self.lanes)]
        return remote(view, view, self.send.at[t], self.recv.at[t], self.partner[self.order[t]])

    def start(self, t):
        self.copy(t, False).start()

    def finish(self, t):
        self.copy(t, True).wait_recv()

    def drain(self):
        for t in range(len(self.order)):
            self.copy(t, False).wait_send()


def imaging_kernel(
    part_ref, kern_mine, target_ref, lh_hbm, ll_hbm, th_hbm, tl_hbm,
    out_ref, resist_ref,
    lh, ll, th, tl, table_sem,
    kbuf, p0, p1, p2, spec, ph, pw, cout, cin, ch, cl, field,
    light, l0, l1, l2, l3, slope, grad, gin, acc, sums, s0, s1, s2, s3,
    ks, kr_, ps, pr_, as_, ar, xs, xr, ls, lr, gs, gr, cs, cr, ss, sr_, os_, or_, fs, fr, us, ur,
):
    H, W, C = G // 2, G // PARTS, B // 2
    sp, kq = lax.axis_index("space"), lax.axis_index("kern")
    z, x = sp // 2, lax.rem(sp, 2)
    y, core = kq // 2, lax.rem(kq, 2)
    me = {"y": y, "h": z // 2, "l": lax.rem(z, 2), "x": x}
    partner = {
        "y": (sp, (1 - y) * 2 + core),
        "x": (z * 2 + 1 - x, kq),
        "l": ((z + 1 - 2 * me["l"]) * 2 + x, kq),
        "h": (lax.rem(z + 2, 4) * 2 + x, kq),
    }
    sibling = (sp, y * 2 + 1 - core)
    lanes = [pl.ds(j * W, W) for j in range(PARTS)]
    tables = [
        pltpu.make_async_copy(src, dst, table_sem.at[i])
        for i, (src, dst) in enumerate(zip((lh_hbm, ll_hbm, th_hbm, tl_hbm), (lh, ll, th, tl)))
    ]
    for t in tables:
        t.start()

    barrier = pltpu.get_barrier_semaphore()
    for device in list(partner.values()) + [sibling]:
        pl.semaphore_signal(barrier, inc=1, device_id=device, device_id_type=MESH)
    half, slot = sp // 4, lax.rem(sp, 4)
    holder = [(core * 4 + k, y * 2 + half) for k in range(4)]
    stays = [jnp.logical_and(half == core, slot == k) for k in range(4)]
    for k in range(4):
        @pl.when(jnp.logical_not(stays[k]))
        def _():
            pl.semaphore_signal(barrier, inc=1, device_id=holder[k], device_id_type=MESH)

    pl.semaphore_wait(barrier, 9 - jnp.where(half == core, 1, 0))

    scatter = [
        Scatter(me, partner, part_ref, (p0, p1, p2), "hlx", SPACE_ORDERS[j], lanes[j], ps.at[j], pr_.at[j])
        for j in range(PARTS)
    ]
    gather = [
        Gather(me, partner, spec, DIMS, ORDERS[j][::-1], lanes[j], as_.at[j], ar.at[j]) for j in range(PARTS)
    ]
    for s in scatter:
        s.start(0)

    def kern_copy(k, place):
        return remote(kern_mine.at[:, k], kbuf.at[:, place], ks.at[k], kr_.at[place], holder[k])

    for k in range(4):
        @pl.when(jnp.logical_not(stays[k]))
        def _():
            kern_copy(k, slot).start()

        @pl.when(stays[k])
        def _():
            kbuf[:, slot] = kern_mine[:, k]

    for t in range(3):
        for s in scatter:
            s.finish(t)
            if t < 2:
                s.start(t + 1)
    for j in range(PARTS):
        spec[index(DIMS, me, lanes[j])] = p2[:, lanes[j]]
        gather[j].start(0)
    for t in range(4):
        for g in gather:
            g.finish(t)
            if t < 3:
                g.start(t + 1)
    for k in range(4):
        @pl.when(jnp.logical_not(stays[k]))
        def _():
            kern_copy(k, k).wait_recv()

    def product(i, c):
        rows = pl.ds(pl.multiple_of(i * 64, 64), 64)
        kr, ki = kbuf[0, i], kbuf[1, i]
        value = spec[i // 2, lax.rem(i, 2)].reshape(64, 2 * B)
        sr, si = value[:, :B], value[:, B:]
        ph[rows, :B], pw[rows, :B] = halves(kr * sr - ki * si)
        ph[rows, B:], pw[rows, B:] = halves(kr * si + ki * sr)
        return c

    lax.fori_loop(0, 4, product, 0)
    tables[0].wait()
    tables[1].wait()

    def lift(d, i):
        rows = pl.ds(pl.multiple_of(i * 256, 256), 256)
        return dot3(lh[d, rows, :], ll[d, rows, :], ph[...], pw[...], NT)

    def cross_copy(i):
        return remote(cout.at[i], cin.at[i], xs.at[i], xr.at[i], sibling)

    def lift_other(i, c):
        cout[i] = lift(1 - core, i)
        cross_copy(i).start()
        return c

    lax.fori_loop(0, 4, lift_other, 0)

    def lift_own(i, c):
        rows = pl.ds(pl.multiple_of(i * 256, 256), 256)
        mine = pl.ds(pl.multiple_of(core * C, C), C)
        ch[rows, mine], cl[rows, mine] = halves(lift(core, i))
        return c

    lax.fori_loop(0, 4, lift_own, 0)

    def cross_land(i, c):
        rows = pl.ds(pl.multiple_of(i * 256, 256), 256)
        other = pl.ds(pl.multiple_of((1 - core) * C, C), C)
        cross_copy(i).wait_recv()
        ch[rows, other], cl[rows, other] = halves(cin[i])
        return c

    lax.fori_loop(0, 4, cross_land, 0)
    tables[2].wait()
    tables[3].wait()

    add_light = [
        Scatter(me, partner, light, (l0, l1, l2, l3), DIMS, ORDERS[j], lanes[j], ls.at[j], lr.at[j])
        for j in range(PARTS)
    ]
    spread = [
        Gather(me, partner, slope, DIMS, ORDERS[j][::-1], lanes[j], gs.at[j], gr.at[j]) for j in range(PARTS)
    ]
    own_rows = pl.ds(pl.multiple_of(core * 64 + y * 32, 32), 32)

    def image(j):
        def chunk(i, c):
            top = pl.ds(pl.multiple_of(i * 256, 256), 256)
            low = pl.ds(pl.multiple_of(H + i * 256, 256), 256)
            a = dot3(ch[top, :], cl[top, :], th[j], tl[j], NN)
            b = dot3(ch[low, :], cl[low, :], th[j], tl[j], NN)
            re = a[:, :W] - b[:, W:]
            im = a[:, W:] + b[:, :W]
            field[top, lanes[j]] = re
            field[low, lanes[j]] = im
            light[i, :, :, :, :, lanes[j]] = (re * re + im * im).reshape(2, 2, 2, 32, W)
            return c

        lax.fori_loop(0, 2, chunk, 0)

    def expose(j):
        intensity = l3[:, lanes[j]] * (1.0 / (B * B))
        resist = jax.nn.sigmoid(steepness * (intensity - threshold))
        resist_ref[own_rows, lanes[j]] = resist
        goal = target_ref[own_rows, lanes[j]].astype(jnp.float32)
        slope[index(DIMS, me, lanes[j])] = (4.0 * steepness / (B * B)) * (resist - goal) * resist * (1.0 - resist)

    def back(j):
        def chunk(i, c):
            top = pl.ds(pl.multiple_of(i * 256, 256), 256)
            low = pl.ds(pl.multiple_of(H + i * 256, 256), 256)
            scale = slope[i, :, :, :, :, lanes[j]].reshape(256, W)
            rh, rl = halves(field[top, lanes[j]] * scale)
            ih, il = halves(field[low, lanes[j]] * scale)
            one = dot3(
                th[j], tl[j], jnp.concatenate([rh, ih], 1), jnp.concatenate([rl, il], 1), NT
            )
            two = dot3(
                th[j], tl[j], jnp.concatenate([ih, -rh], 1), jnp.concatenate([il, -rl], 1), NT
            )
            if j == 0:
                grad[:, top] = one
                grad[:, low] = two
            else:
                grad[:, top] = grad[:, top] + one
                grad[:, low] = grad[:, low] + two
            return c

        lax.fori_loop(0, 2, chunk, 0)

    for tick in range(PARTS + 9):
        if tick < PARTS:
            image(tick)
            add_light[tick].start(0)
        for j in range(PARTS):
            s = tick - j
            if 1 <= s <= 4:
                add_light[j].finish(s - 1)
                if s < 4:
                    add_light[j].start(s)
                else:
                    expose(j)
                    spread[j].start(0)
            elif 5 <= s <= 8:
                spread[j].finish(s - 5)
                if s < 8:
                    spread[j].start(s - 4)
        if 0 <= tick - 8 < PARTS:
            back(tick - 8)

    def resist_copy(i, rows, device):
        return remote(resist_ref.at[rows], resist_ref.at[rows], us.at[i], ur.at[i], device)

    row_of = lambda c, yy: pl.ds(pl.multiple_of(c * 64 + yy * 32, 32), 32)
    resist_copy(0, row_of(core, y), partner["y"]).start()
    resist_copy(1, row_of(core, y), sibling).start()

    def grad_copy():
        rows = pl.ds(pl.multiple_of((1 - core) * C, C), C)
        return remote(grad.at[rows], gin, cs, cr, sibling)

    grad_copy().start()

    def adjoint(value, d, first):
        dh, dl = halves(value)

        def chunk(i, c):
            cols = pl.ds(pl.multiple_of(i * 256, 256), 256)
            piece = dot3(dh, dl, lh[d, :, cols], ll[d, :, cols], NN)
            acc[:, cols] = piece if first else acc[:, cols] + piece
            return c

        lax.fori_loop(0, 4, chunk, 0)

    adjoint(grad[pl.ds(pl.multiple_of(core * C, C), C), :], core, True)
    grad_copy().wait_recv()
    adjoint(gin[...], 1 - core, False)

    def combine(i, c):
        rows = pl.ds(pl.multiple_of(i * 64, 64), 64)
        kr, ki = kbuf[0, i], kbuf[1, i]
        pr, pi = acc[rows, :B], acc[rows, B:]
        sums[i // 2, lax.rem(i, 2), :, :, :, :B] = (kr * pr + ki * pi).reshape(2, 2, 16, B)
        sums[i // 2, lax.rem(i, 2), :, :, :, B:] = (kr * pi - ki * pr).reshape(2, 2, 16, B)
        return c

    lax.fori_loop(0, 4, combine, 0)
    add_sums = [
        Scatter(me, partner, sums, (s0, s1, s2, s3), DIMS, ORDERS[j], lanes[j], ss.at[j], sr_.at[j])
        for j in range(PARTS)
    ]
    out_mine = out_ref.at[core]
    deliver = [
        Gather(me, partner, out_mine, DIMS, ORDERS[j][::-1], lanes[j], os_.at[j], or_.at[j]) for j in range(PARTS)
    ]
    for s in add_sums:
        s.start(0)
    for t in range(4):
        for j, s in enumerate(add_sums):
            s.finish(t)
            if t < 3:
                s.start(t + 1)
            else:
                out_ref[(core,) + index(DIMS, me, lanes[j])] = s3[:, lanes[j]]
                deliver[j].start(0)

    def final_copy(j, c):
        view = out_ref.at[(c,) + index(DIMS, {}, lanes[j])]
        return remote(view, view, fs.at[j], fr.at[j], sibling)

    for t in range(4):
        for j, g in enumerate(deliver):
            g.finish(t)
            if t < 3:
                g.start(t + 1)
            else:
                final_copy(j, core).start()
    resist_copy(0, row_of(core, 1 - y), partner["y"]).wait_recv()
    resist_copy(2, row_of(core, 1 - y), sibling).start()
    resist_copy(1, row_of(1 - core, y), sibling).wait_recv()
    resist_copy(2, row_of(1 - core, 1 - y), sibling).wait_recv()
    for j in range(PARTS):
        final_copy(j, 1 - core).wait_recv()

    for j in range(PARTS):
        final_copy(j, core).wait_send()
    for group in (scatter, gather, add_light, spread, add_sums, deliver):
        for one in group:
            one.drain()
    for k in range(4):
        @pl.when(jnp.logical_not(stays[k]))
        def _():
            kern_copy(k, slot).wait_send()

    for i in range(4):
        cross_copy(i).wait_send()
    grad_copy().wait_send()
    resist_copy(0, row_of(core, y), partner["y"]).wait_send()
    resist_copy(1, row_of(core, y), sibling).wait_send()
    resist_copy(2, row_of(core, 1 - y), sibling).wait_send()


def call(kernel, outs, specs, scratch, cid, args, mib):
    vm = pl.BlockSpec(memory_space=pltpu.VMEM)
    return pl.pallas_call(
        kernel,
        out_shape=outs,
        in_specs=specs,
        out_specs=jax.tree.map(lambda _: vm, outs),
        scratch_shapes=scratch,
        compiler_params=pltpu.CompilerParams(
            collective_id=cid, has_side_effects=True, vmem_limit_bytes=mib * 2**20
        ),
    )(*args)


def fast(S, Q, mask, kernels, target):
    f32, bf16 = jnp.float32, jnp.bfloat16
    R = N // S
    DMA = pltpu.SemaphoreType.DMA
    vm, any_ = pl.BlockSpec(memory_space=pltpu.VMEM), pl.BlockSpec(memory_space=pl.ANY)
    high = lax.Precision.HIGH
    sp, kq = lax.axis_index("space"), lax.axis_index("kern")
    table = pixel_table()
    C = B // Q

    rows = jnp.concatenate([lax.dynamic_slice_in_dim(table, part * B + crossed(kq) * C, C, 0) for part in range(2)], axis=0)
    columns = lax.dot_general(rows, mask.astype(f32), (((1,), (1,)), ((), ())), precision=high)
    slab = lax.dynamic_slice_in_dim(table, sp * R, R, 1) * (1.0 / N)
    t = lax.dot_general(columns, slab, (((1,), (1,)), ((), ())), precision=high)
    part = jnp.concatenate([t[:C, :B] - t[C:, B:], t[:C, B:] + t[C:, :B]], axis=1)

    consts = coarse_tables()
    V = pltpu.VMEM
    two = (2, 2, 2, 2)
    total, resist = call(
        imaging_kernel,
        (jax.ShapeDtypeStruct((2,) + two + (16, 2 * B), f32), jax.ShapeDtypeStruct((G // S, G), f32)),
        [vm, vm, vm] + [any_] * 4,
        [V(c.shape, bf16) for c in consts] + [DMA((4,))] + [
            V((2, 4, 64, B), f32),
            V((2, 2, 16, 2 * B), f32), V((2, 16, 2 * B), f32), V((16, 2 * B), f32),
            V(two + (16, 2 * B), f32),
            V((B // 2, 2 * B), bf16), V((B // 2, 2 * B), bf16),
            V((4, 256, B // 2), f32), V((4, 256, B // 2), f32),
            V((G, B), bf16), V((G, B), bf16), V((G, G), f32),
            V(two + (32, G), f32), V((2, 2, 2, 32, G), f32), V((2, 2, 32, G), f32), V((2, 32, G), f32), V((32, G), f32),
            V(two + (32, G), f32),
            V((B, G), f32), V((B // 2, G), f32), V((B // 2, 2 * B), f32),
            V(two + (16, 2 * B), f32), V((2, 2, 2, 16, 2 * B), f32), V((2, 2, 16, 2 * B), f32), V((2, 16, 2 * B), f32),
            V((16, 2 * B), f32),
            DMA((4,)), DMA((4,)), DMA((PARTS, 3)), DMA((PARTS, 3)), DMA((PARTS, 4)), DMA((PARTS, 4)),
            DMA((4,)), DMA((4,)), DMA((PARTS, 4)), DMA((PARTS, 4)), DMA((PARTS, 4)), DMA((PARTS, 4)),
            DMA, DMA, DMA((PARTS, 4)), DMA((PARTS, 4)), DMA((PARTS, 4)), DMA((PARTS, 4)),
            DMA((PARTS,)), DMA((PARTS,)), DMA((3,)), DMA((3,)),
        ],
        1, (part.reshape(2, 2, 2, 16, 2 * B), kernels, target) + consts, 58,
    )

    total = total.reshape(B, 2 * B)
    a, b = slab[:B], slab[B:]
    delta = jnp.concatenate([
        jnp.dot(total, slab, precision=high),
        jnp.dot(total, jnp.concatenate([-b, a], axis=0), precision=high),
    ], axis=0)
    gradient = lax.dot_general(lax.optimization_barrier(delta), table, (((0,), (0,)), ((), ())), precision=high)
    return gradient, resist


def solution(mesh):
    in_specs = (P("space", None), P(None, "kern", "space", None), P("space", None))
    out_specs = (P("space", None), P("space", None))
    S, Q = mesh.shape["space"], mesh.shape["kern"]
    body = functools.partial(fast, S, Q) if (S, Q) == (8, 4) else local
    return jax.shard_map(body, mesh=mesh, in_specs=in_specs, out_specs=out_specs, check_vma=False)
```

time: 232 us -> 205 us (0.88)
  Pallas kernels: 188 us -> 164 us
    pallas_call x1, Pallas kernels: 188 us -> 164 us  [call(): pl.pallas_call(kernel, out_shape=outs, in_specs=specs, out_specs=jax.tree...]
where the time goes in v1:
time: 205 us; the launch traced here: 204 us
  Pallas kernels  164 us (80%)
  matrix products  32.2 us (16%)
  local copies, waits for them, and re-layouts  4.24 us (2%)
  other arithmetic  3.12 us (2%)
    pallas_call x1, Pallas kernels, call(): pl.pallas_call(kernel, out_shape=outs, in_specs=specs, out_specs=jax.tree...  164 us
    dot_general x1, matrix products, fast(): lax.dot_general(lax.optimization_barrier(delta), table, (((0,), (0,)), ((...  20 us

profile of v1, /device:TPU:1, one launch (start us, length us, event | category | flops | bytes accessed | tf_op | source)
XLA Modules:
  0.0 204.5 jit_solution(15223664954496404825)
XLA Ops:
  0.7 1.8 dynamic-slice_multiply_fusion
  2.5 0.2 slice_negate_fusion
  2.7 0.0 copy-start.1
  2.7 2.7 %constant_dynamic-slice_fusion.1 = (f32[128,4096]{1,0:T(8,128)S(1)}, f32[128,4096]{1,0:T(8,128)S(1)}) fusion(f32[1024,4096]{1,0:T(8,128)} %constant.49.clone, s32[]{:T(128)S(6)} %select_n.16, s32[]{:T(128)S(6)} %select_n.17), kind=kLoop, calls=%fused_computation.21 | loop fusion | bytes 8388616 | tf_op jit(solution)/shard_map/dynamic_slice | solution.py:633
  5.4 0.8 copy-done.1
  6.2 2.4 %fusion = f32[256,512]{1,0:T(8,128)S(1)} fusion(bf16[512,4096]{1,0:T(8,128)(2,1)S(1)} %copy-done.1, f32[128,4096]{1,0:T(8,128)S(1)} %get-tuple-element.7, f32[128,4096]{1,0:T(8,128)S(1)} %get-tuple-element.6), kind=kOutput, calls=%fused_computation | convolution fusion | flops 3222274048 | bytes 8912896 | tf_op jit(solution)/shard_map/dot_general | solution.py:634
  8.5 2.7 %fusion.9 = f32[256,1024]{1,0:T(8,128)S(1)} fusion(f32[256,512]{1,0:T(8,128)S(1)} %fusion, f32[1024,4096]{1,0:T(8,128)} %constant.49.clone, s32[]{:T(128)S(6)} %select_n.18), kind=kOutput, calls=%fused_computation.11 | convolution fusion | flops 805830656 | bytes 3670020 | tf_op jit(solution)/shard_map/dot_general | solution.py:636
  11.3 0.1 slice_subtract_fusion
  11.3 0.8 pad_maximum_fusion.1
  12.2 164.1 %shard_map.95 = (f32[2,2,2,2,2,16,1024]{6,5,4,3,2,1,0:T(8,128)}, f32[128,1024]{1,0:T(8,128)}) custom-call(f32[2,2,2,16,1024]{4,3,2,1,0:T(8,128)} %bitcast.10, f32[2,4,64,512]{3,2,1,0:T(8,128)} %kern_mine.1, s32[128,1024]{1,0:T(8,128)} %target_ref.1, bf16[2,1024,1024]{2,1,0:T(8,128)(2,1)} %constant.50.clone.lh_hbm, ...), custom_call_target="tpu_custom_call" | custom-call | tf_op jit(solution)/shard_map/pallas_call | solution.py:611
  176.3 0.0 copy-start
  176.3 3.6 %fusion.4 = f32[512,512]{1,0:T(8,128)S(1)} fusion(f32[512,1024]{1,0:T(8,128)} %bitcast.8, f32[512,512]{1,0:T(8,128)S(1)} %get-tuple-element.9, f32[512,512]{1,0:T(8,128)S(1)} %get-tuple-element.8), kind=kOutput, calls=%fused_computation.4 | convolution fusion | flops 1611137024 | bytes 5242880 | tf_op jit(solution)/shard_map/dot_general | solution.py:670
  179.9 0.0 copy-done
  179.9 3.5 %fusion.8 = f32[512,512]{1,0:T(8,128)S(1)} fusion(f32[512,1024]{1,0:T(8,128)S(1)} %bitcast.9, f32[1024,4096]{1,0:T(8,128)} %constant.49.clone, s32[]{:T(128)S(6)} %select_n.18), kind=kOutput, calls=%fused_computation.10 | convolution fusion | flops 1611137024 | bytes 5242884 | tf_op jit(solution)/shard_map/dot_general | solution.py:669
  183.4 0.2 pad_maximum_fusion
  183.6 0.0 copy-start.2
  183.6 20.0 %fusion.18 = f32[512,4096]{1,0:T(8,128)} fusion(f32[1024,512]{1,0:T(8,128)S(1)} %pad_maximum_fusion, f32[1024,4096]{1,0:T(8,128)} %constant.49.clone), kind=kOutput, calls=%fused_computation.26 | convolution fusion | flops 12884901888 | bytes 27262976 | tf_op jit(solution)/shard_map/dot_general | solution.py:672
  203.7 0.0 copy-done.2
  203.7 0.8 copy.11
Async XLA Ops:
  2.7 3.5 %copy-start.1 = (bf16[512,4096]{1,0:T(8,128)(2,1)S(1)}, bf16[512,4096]{1,0:T(8,128)(2,1)}, u32[]{:S(2)}) copy-start(bf16[512,4096]{1,0:T(8,128)(2,1)} %param.8) | copy-start | bytes 12582916
  176.3 3.6 %copy-start = (f32[2,2,2,2,2,16,1024]{6,5,4,3,2,1,0:T(8,128)S(1)}, f32[2,2,2,2,2,16,1024]{6,5,4,3,2,1,0:T(8,128)}, u32[]{:S(2)}) copy-start(f32[2,2,2,2,2,16,1024]{6,5,4,3,2,1,0:T(8,128)} %get-tuple-element.4) | copy-start | bytes 6291460
  183.6 20.0 %copy-start.2 = (f32[128,1024]{1,0:T(8,128)S(1)}, f32[128,1024]{1,0:T(8,128)}, u32[]{:S(2)}) copy-start(f32[128,1024]{1,0:T(8,128)} %get-tuple-element.15) | copy-start | bytes 1572868

commit v2 on v1

--- a/solution.py
+++ b/solution.py
@@ -206,10 +206,13 @@
     return jnp.asarray(high), jnp.asarray(low)
 
 
-def pixel_table():
+def pixel_tables():
     f = np.arange(B) - B // 2
     angle = (f[:, None] * np.arange(N)) % N * (2 * np.pi / N)
-    return jnp.asarray(np.concatenate([np.cos(angle), -np.sin(angle)]).astype(np.float32))
+    c, s = np.cos(angle), -np.sin(angle)
+    blocks = np.concatenate([c.reshape(B // BLOCK, BLOCK, N), s.reshape(B // BLOCK, BLOCK, N)], 1)
+    parity = np.stack([np.concatenate([c[p::2, : N // 2], s[p::2, : N // 2]]) for p in range(2)])
+    return split_constant(blocks), split_constant(parity)
 
 
 def coarse_tables():
@@ -219,8 +222,8 @@
     c, s = np.cos(angle), np.sin(angle)
     order = np.arange(G).reshape(8, 2, 2, G // 32).transpose(1, 2, 0, 3).reshape(2, G // 2)
     lift = np.stack([np.block([[c.T[o], -s.T[o]], [s.T[o], c.T[o]]]) for o in order])
-    W = G // PARTS
-    image = np.stack([np.concatenate([c[:, j * W : j * W + W], s[:, j * W : j * W + W]], 1) for j in range(PARTS)])
+    W = G // STRIPS
+    image = np.stack([np.concatenate([c[:, j * W : j * W + W], s[:, j * W : j * W + W]], 1) for j in range(STRIPS)])
     return split_constant(lift) + split_constant(image)
 
 
@@ -237,8 +240,13 @@
 NN = ((1,), (0,))
 NT = ((1,), (1,))
 PARTS = 4
+BLOCK = 128
+STRIPS = 8
+STRIP_ORDERS = ("xylh", "ylxh", "lxyh", "xylh", "ylxh", "lxyh", "xylh", "ylxh")
+SUM_TIMES = (4, 7, 9, 11)
+SPREAD_TIMES = (13, 15, 18, 22)
 DIMS = "yhlx"
-ORDERS = ("xylh", "ylxh", "lxyh", "yxlh")
+ORDERS = ("xylh", "ylxh", "lxyh", "xylh")
 SPACE_ORDERS = ("xlh", "lxh", "xlh", "lxh")
 
 
@@ -314,14 +322,14 @@
 
 
 def imaging_kernel(
-    part_ref, kern_mine, target_ref, lh_hbm, ll_hbm, th_hbm, tl_hbm,
+    mask_hbm, kern_mine, target_hbm, bh_hbm, bl_hbm, lh_hbm, ll_hbm, th_hbm, tl_hbm,
     out_ref, resist_ref,
-    lh, ll, th, tl, table_sem,
+    lh, ll, th, tl, table_sem, mbuf, fh, fl, load_sem, slabh, slabl, target_ref, slab_sem, columns, part_ref,
     kbuf, p0, p1, p2, spec, ph, pw, cout, cin, ch, cl, field,
     light, l0, l1, l2, l3, slope, grad, gin, acc, sums, s0, s1, s2, s3,
     ks, kr_, ps, pr_, as_, ar, xs, xr, ls, lr, gs, gr, cs, cr, ss, sr_, os_, or_, fs, fr, us, ur,
 ):
-    H, W, C = G // 2, G // PARTS, B // 2
+    H, W, C = G // 2, G // STRIPS, B // 2
     sp, kq = lax.axis_index("space"), lax.axis_index("kern")
     z, x = sp // 2, lax.rem(sp, 2)
     y, core = kq // 2, lax.rem(kq, 2)
@@ -333,12 +341,27 @@
         "h": (lax.rem(z + 2, 4) * 2 + x, kq),
     }
     sibling = (sp, y * 2 + 1 - core)
-    lanes = [pl.ds(j * W, W) for j in range(PARTS)]
+    lanes = [pl.ds(j * (2 * B // PARTS), 2 * B // PARTS) for j in range(PARTS)]
+    strips = [pl.ds(j * W, W) for j in range(STRIPS)]
+    span = N // 4
+    loads = []
+    for i in range(4):
+        cols = pl.ds(i * span, span)
+        blk = 2 * core + y
+        pairs = [(mask_hbm.at[:, cols], mbuf.at[i]), (bh_hbm.at[blk, :, cols], fh.at[i]), (bl_hbm.at[blk, :, cols], fl.at[i])]
+        loads.append([pltpu.make_async_copy(a, b, load_sem.at[i, n]) for n, (a, b) in enumerate(pairs)])
+    rows_mine = pl.ds(pl.multiple_of(sp * (N // 8), N // 8), N // 8)
+    others = [
+        pltpu.make_async_copy(a, b, slab_sem.at[n])
+        for n, (a, b) in enumerate(
+            [(bh_hbm.at[:, :, rows_mine], slabh), (bl_hbm.at[:, :, rows_mine], slabl), (target_hbm, target_ref)]
+        )
+    ]
     tables = [
         pltpu.make_async_copy(src, dst, table_sem.at[i])
         for i, (src, dst) in enumerate(zip((lh_hbm, ll_hbm, th_hbm, tl_hbm), (lh, ll, th, tl)))
     ]
-    for t in tables:
+    for t in sum(loads, []) + others + tables:
         t.start()
 
     barrier = pltpu.get_barrier_semaphore()
@@ -361,20 +384,45 @@
     gather = [
         Gather(me, partner, spec, DIMS, ORDERS[j][::-1], lanes[j], as_.at[j], ar.at[j]) for j in range(PARTS)
     ]
-    for s in scatter:
-        s.start(0)
-
     def kern_copy(k, place):
         return remote(kern_mine.at[:, k], kbuf.at[:, place], ks.at[k], kr_.at[place], holder[k])
 
-    for k in range(4):
+    def kern_stay(k):
+        return pltpu.make_async_copy(kern_mine.at[:, k], kbuf.at[:, k], kr_.at[k])
+
+    def kern_send(k):
         @pl.when(jnp.logical_not(stays[k]))
         def _():
             kern_copy(k, slot).start()
 
         @pl.when(stays[k])
         def _():
-            kbuf[:, slot] = kern_mine[:, k]
+            kern_stay(k).start()
+
+    kern_send(0)
+    kern_send(1)
+
+    for i in range(4):
+        for t in loads[i]:
+            t.wait()
+        m = mbuf[i]
+        d = functools.partial(lax.dot_general, dimension_numbers=(NT, ((), ())), preferred_element_type=jnp.float32)
+        piece = d(fh[i], m) + d(fl[i], m)
+        columns[...] = piece if i == 0 else columns[...] + piece
+    for t in others[:2]:
+        t.wait()
+    colh, coll = halves(columns[...] * (1.0 / N))
+    for j in range(PARTS):
+        for i in range(2):
+            n = j % 2 * 2 + i
+            value = dot3(colh, coll, slabh[n], slabl[n], NT)
+            if j < 2:
+                value = value[:BLOCK, :BLOCK] - value[BLOCK:, BLOCK:]
+            else:
+                value = value[:BLOCK, BLOCK:] + value[BLOCK:, :BLOCK]
+            part_ref[:, :, :, :, pl.ds((2 * j + i) * BLOCK, BLOCK)] = value.reshape(2, 2, 2, 16, BLOCK)
+        scatter[j].start(0)
+    kern_send(2)
 
     for t in range(3):
         for s in scatter:
@@ -384,6 +432,7 @@
     for j in range(PARTS):
         spec[index(DIMS, me, lanes[j])] = p2[:, lanes[j]]
         gather[j].start(0)
+    kern_send(3)
     for t in range(4):
         for g in gather:
             g.finish(t)
@@ -394,6 +443,10 @@
         def _():
             kern_copy(k, k).wait_recv()
 
+        @pl.when(stays[k])
+        def _():
+            kern_stay(k).wait()
+
     def product(i, c):
         rows = pl.ds(pl.multiple_of(i * 64, 64), 64)
         kr, ki = kbuf[0, i], kbuf[1, i]
@@ -441,11 +494,11 @@
     tables[3].wait()
 
     add_light = [
-        Scatter(me, partner, light, (l0, l1, l2, l3), DIMS, ORDERS[j], lanes[j], ls.at[j], lr.at[j])
-        for j in range(PARTS)
+        Scatter(me, partner, light, (l0, l1, l2, l3), DIMS, STRIP_ORDERS[j], strips[j], ls.at[j], lr.at[j])
+        for j in range(STRIPS)
     ]
     spread = [
-        Gather(me, partner, slope, DIMS, ORDERS[j][::-1], lanes[j], gs.at[j], gr.at[j]) for j in range(PARTS)
+        Gather(me, partner, slope, DIMS, STRIP_ORDERS[j][::-1], strips[j], gs.at[j], gr.at[j]) for j in range(STRIPS)
     ]
     own_rows = pl.ds(pl.multiple_of(core * 64 + y * 32, 32), 32)
 
@@ -457,27 +510,27 @@
             b = dot3(ch[low, :], cl[low, :], th[j], tl[j], NN)
             re = a[:, :W] - b[:, W:]
             im = a[:, W:] + b[:, :W]
-            field[top, lanes[j]] = re
-            field[low, lanes[j]] = im
-            light[i, :, :, :, :, lanes[j]] = (re * re + im * im).reshape(2, 2, 2, 32, W)
+            field[top, strips[j]] = re
+            field[low, strips[j]] = im
+            light[i, :, :, :, :, strips[j]] = (re * re + im * im).reshape(2, 2, 2, 32, W)
             return c
 
         lax.fori_loop(0, 2, chunk, 0)
 
     def expose(j):
-        intensity = l3[:, lanes[j]] * (1.0 / (B * B))
+        intensity = l3[:, strips[j]] * (1.0 / (B * B))
         resist = jax.nn.sigmoid(steepness * (intensity - threshold))
-        resist_ref[own_rows, lanes[j]] = resist
-        goal = target_ref[own_rows, lanes[j]].astype(jnp.float32)
-        slope[index(DIMS, me, lanes[j])] = (4.0 * steepness / (B * B)) * (resist - goal) * resist * (1.0 - resist)
+        resist_ref[own_rows, strips[j]] = resist
+        goal = target_ref[own_rows, strips[j]].astype(jnp.float32)
+        slope[index(DIMS, me, strips[j])] = (4.0 * steepness / (B * B)) * (resist - goal) * resist * (1.0 - resist)
 
     def back(j):
         def chunk(i, c):
             top = pl.ds(pl.multiple_of(i * 256, 256), 256)
             low = pl.ds(pl.multiple_of(H + i * 256, 256), 256)
-            scale = slope[i, :, :, :, :, lanes[j]].reshape(256, W)
-            rh, rl = halves(field[top, lanes[j]] * scale)
-            ih, il = halves(field[low, lanes[j]] * scale)
+            scale = slope[i, :, :, :, :, strips[j]].reshape(256, W)
+            rh, rl = halves(field[top, strips[j]] * scale)
+            ih, il = halves(field[low, strips[j]] * scale)
             one = dot3(
                 th[j], tl[j], jnp.concatenate([rh, ih], 1), jnp.concatenate([rl, il], 1), NT
             )
@@ -494,25 +547,34 @@
 
         lax.fori_loop(0, 2, chunk, 0)
 
-    for tick in range(PARTS + 9):
-        if tick < PARTS:
-            image(tick)
-            add_light[tick].start(0)
-        for j in range(PARTS):
-            s = tick - j
-            if 1 <= s <= 4:
-                add_light[j].finish(s - 1)
-                if s < 4:
-                    add_light[j].start(s)
-                else:
-                    expose(j)
-                    spread[j].start(0)
-            elif 5 <= s <= 8:
-                spread[j].finish(s - 5)
-                if s < 8:
-                    spread[j].start(s - 4)
-        if 0 <= tick - 8 < PARTS:
-            back(tick - 8)
+    def show(j):
+        image(j)
+        add_light[j].start(0)
+
+    def add_step(j, t):
+        add_light[j].finish(t)
+        if t < 3:
+            add_light[j].start(t + 1)
+        else:
+            expose(j)
+            spread[j].start(0)
+
+    def spread_step(j, t):
+        spread[j].finish(t)
+        if t < 3:
+            spread[j].start(t + 1)
+        else:
+            back(j)
+
+    events = []
+    for j in range(STRIPS):
+        events.append((j, 0, j, functools.partial(show, j)))
+        for t in range(4):
+            events.append((j + SUM_TIMES[t], 2, j, functools.partial(add_step, j, t)))
+            events.append((j + SPREAD_TIMES[t], 3 if t == 3 else 1, j, functools.partial(spread_step, j, t)))
+    others[2].wait()
+    for event in sorted(events, key=lambda e: e[:3]):
+        event[3]()
 
     def resist_copy(i, rows, device):
         return remote(resist_ref.at[rows], resist_ref.at[rows], us.at[i], ur.at[i], device)
@@ -527,40 +589,32 @@
 
     grad_copy().start()
 
-    def adjoint(value, d, first):
-        dh, dl = halves(value)
-
-        def chunk(i, c):
-            cols = pl.ds(pl.multiple_of(i * 256, 256), 256)
-            piece = dot3(dh, dl, lh[d, :, cols], ll[d, :, cols], NN)
-            acc[:, cols] = piece if first else acc[:, cols] + piece
-            return c
-
-        lax.fori_loop(0, 4, chunk, 0)
-
-    adjoint(grad[pl.ds(pl.multiple_of(core * C, C), C), :], core, True)
+    def adjoint(dh, dl, d, cols):
+        return dot3(dh, dl, lh[d, :, cols], ll[d, :, cols], NN)
+
+    gh, gl = halves(grad[pl.ds(pl.multiple_of(core * C, C), C), :])
+    for cols in lanes:
+        acc[:, cols] = adjoint(gh, gl, core, cols)
     grad_copy().wait_recv()
-    adjoint(gin[...], 1 - core, False)
-
-    def combine(i, c):
-        rows = pl.ds(pl.multiple_of(i * 64, 64), 64)
-        kr, ki = kbuf[0, i], kbuf[1, i]
-        pr, pi = acc[rows, :B], acc[rows, B:]
-        sums[i // 2, lax.rem(i, 2), :, :, :, :B] = (kr * pr + ki * pi).reshape(2, 2, 16, B)
-        sums[i // 2, lax.rem(i, 2), :, :, :, B:] = (kr * pi - ki * pr).reshape(2, 2, 16, B)
-        return c
-
-    lax.fori_loop(0, 4, combine, 0)
+    gh, gl = halves(gin[...])
     add_sums = [
         Scatter(me, partner, sums, (s0, s1, s2, s3), DIMS, ORDERS[j], lanes[j], ss.at[j], sr_.at[j])
         for j in range(PARTS)
     ]
+    for j in range(2):
+        cols = lanes[j]
+        pr = acc[:, lanes[j]] + adjoint(gh, gl, 1 - core, lanes[j])
+        pi = acc[:, lanes[j + 2]] + adjoint(gh, gl, 1 - core, lanes[j + 2])
+        kr = kbuf[0, :, :, lanes[j]].reshape(C, C)
+        ki = kbuf[1, :, :, lanes[j]].reshape(C, C)
+        sums[:, :, :, :, :, lanes[j]] = (kr * pr + ki * pi).reshape(2, 2, 2, 2, 16, C)
+        add_sums[j].start(0)
+        sums[:, :, :, :, :, lanes[j + 2]] = (kr * pi - ki * pr).reshape(2, 2, 2, 2, 16, C)
+        add_sums[j + 2].start(0)
     out_mine = out_ref.at[core]
     deliver = [
         Gather(me, partner, out_mine, DIMS, ORDERS[j][::-1], lanes[j], os_.at[j], or_.at[j]) for j in range(PARTS)
     ]
-    for s in add_sums:
-        s.start(0)
     for t in range(4):
         for j, s in enumerate(add_sums):
             s.finish(t)
@@ -620,30 +674,80 @@
     )(*args)
 
 
+def final_kernel(
+    total_ref, bh_hbm, bl_hbm, eh_hbm, el_hbm, out_hbm, slabh, slabl, eh, el, split, dh, dl, stage, slab_sem, table_sem, out_sem
+):
+    R, W, H = N // 8, 256, N // 2
+    sp = lax.axis_index("space")
+    rows = pl.ds(pl.multiple_of(sp * R, R), R)
+    slabs = [
+        pltpu.make_async_copy(src.at[:, :, rows], dst, slab_sem.at[i])
+        for i, (src, dst) in enumerate(((bh_hbm, slabh), (bl_hbm, slabl)))
+    ]
+    tables = [
+        pltpu.make_async_copy(src, dst, table_sem.at[i]) for i, (src, dst) in enumerate(((eh_hbm, eh), (el_hbm, el)))
+    ]
+    for t in slabs:
+        t.start()
+    for i in range(2 * B // BLOCK):
+        split[i] = total_ref[:, pl.ds(i * BLOCK, BLOCK)] * (1.0 / N)
+    for t in slabs:
+        t.wait()
+    for t in tables:
+        t.start()
+    sh, sl = slabh[...].reshape(2 * B, R), slabl[...].reshape(2 * B, R)
+    groups = B // BLOCK
+    for p in range(2):
+        re = [split[i, pl.ds(p, B // 2, stride=2), :] for i in range(groups)]
+        im = [split[groups + i, pl.ds(p, B // 2, stride=2), :] for i in range(groups)]
+        re, im = [halves(v) for v in re], [halves(v) for v in im]
+        for side in range(2):
+            pick = lambda n: jnp.concatenate(
+                sum([[re[i][n], im[i][n]] if side == 0 else [im[i][n], -re[i][n]] for i in range(groups)], []), axis=1
+            )
+            value = dot3(pick(0), pick(1), sh, sl, NN)
+            cols = pl.ds(side * (B // 2), B // 2)
+            dh[p, :, cols], dl[p, :, cols] = halves(value.T)
+    for t in tables:
+        t.wait()
+
+    def out_copy(i, half):
+        slot = i % 2
+        return pltpu.make_async_copy(
+            stage.at[slot, half], out_hbm.at[:, pl.ds(half * H + i * W, W)], out_sem.at[slot, half]
+        )
+
+    for i in range(H // W):
+        cols = pl.ds(i * W, W)
+        even = dot3(dh[0], dl[0], eh[0, :, cols], el[0, :, cols], NN)
+        odd = dot3(dh[1], dl[1], eh[1, :, cols], el[1, :, cols], NN)
+        for half in range(2):
+            if i >= 2:
+                out_copy(i - 2, half).wait()
+            stage[i % 2, half] = even + odd if half == 0 else even - odd
+            out_copy(i, half).start()
+    for i in range(H // W - 2, H // W):
+        for half in range(2):
+            out_copy(i, half).wait()
+
+
 def fast(S, Q, mask, kernels, target):
     f32, bf16 = jnp.float32, jnp.bfloat16
-    R = N // S
+    R, groups = N // S, B // BLOCK
     DMA = pltpu.SemaphoreType.DMA
-    vm, any_ = pl.BlockSpec(memory_space=pltpu.VMEM), pl.BlockSpec(memory_space=pl.ANY)
-    high = lax.Precision.HIGH
-    sp, kq = lax.axis_index("space"), lax.axis_index("kern")
-    table = pixel_table()
-    C = B // Q
-
-    rows = jnp.concatenate([lax.dynamic_slice_in_dim(table, part * B + crossed(kq) * C, C, 0) for part in range(2)], axis=0)
-    columns = lax.dot_general(rows, mask.astype(f32), (((1,), (1,)), ((), ())), precision=high)
-    slab = lax.dynamic_slice_in_dim(table, sp * R, R, 1) * (1.0 / N)
-    t = lax.dot_general(columns, slab, (((1,), (1,)), ((), ())), precision=high)
-    part = jnp.concatenate([t[:C, :B] - t[C:, B:], t[:C, B:] + t[C:, :B]], axis=1)
-
+    any_ = pl.BlockSpec(memory_space=pl.ANY)
+    blocks, parity = pixel_tables()
     consts = coarse_tables()
     V = pltpu.VMEM
     two = (2, 2, 2, 2)
+    slab = [V((groups, 2 * BLOCK, R), bf16)] * 2
     total, resist = call(
         imaging_kernel,
         (jax.ShapeDtypeStruct((2,) + two + (16, 2 * B), f32), jax.ShapeDtypeStruct((G // S, G), f32)),
-        [vm, vm, vm] + [any_] * 4,
+        [any_] * 9,
         [V(c.shape, bf16) for c in consts] + [DMA((4,))] + [
+            V((4, R, N // 4), bf16), V((4, 2 * BLOCK, N // 4), bf16), V((4, 2 * BLOCK, N // 4), bf16), DMA((4, 3)),
+        ] + slab + [V((G // S, G), jnp.int32), DMA((3,)), V((2 * BLOCK, R), f32), V((2, 2, 2, 16, 2 * B), f32)] + [
             V((2, 4, 64, B), f32),
             V((2, 2, 16, 2 * B), f32), V((2, 16, 2 * B), f32), V((16, 2 * B), f32),
             V(two + (16, 2 * B), f32),
@@ -656,20 +760,22 @@
             V(two + (16, 2 * B), f32), V((2, 2, 2, 16, 2 * B), f32), V((2, 2, 16, 2 * B), f32), V((2, 16, 2 * B), f32),
             V((16, 2 * B), f32),
             DMA((4,)), DMA((4,)), DMA((PARTS, 3)), DMA((PARTS, 3)), DMA((PARTS, 4)), DMA((PARTS, 4)),
-            DMA((4,)), DMA((4,)), DMA((PARTS, 4)), DMA((PARTS, 4)), DMA((PARTS, 4)), DMA((PARTS, 4)),
+            DMA((4,)), DMA((4,)), DMA((STRIPS, 4)), DMA((STRIPS, 4)), DMA((STRIPS, 4)), DMA((STRIPS, 4)),
             DMA, DMA, DMA((PARTS, 4)), DMA((PARTS, 4)), DMA((PARTS, 4)), DMA((PARTS, 4)),
             DMA((PARTS,)), DMA((PARTS,)), DMA((3,)), DMA((3,)),
         ],
-        1, (part.reshape(2, 2, 2, 16, 2 * B), kernels, target) + consts, 58,
-    )
-
-    total = total.reshape(B, 2 * B)
-    a, b = slab[:B], slab[B:]
-    delta = jnp.concatenate([
-        jnp.dot(total, slab, precision=high),
-        jnp.dot(total, jnp.concatenate([-b, a], axis=0), precision=high),
-    ], axis=0)
-    gradient = lax.dot_general(lax.optimization_barrier(delta), table, (((0,), (0,)), ((), ())), precision=high)
+        1, (mask, kernels, target) + blocks + consts, 59,
+    )
+    gradient = pl.pallas_call(
+        final_kernel,
+        out_shape=jax.ShapeDtypeStruct((R, N), f32),
+        in_specs=[pl.BlockSpec(memory_space=pltpu.VMEM)] + [any_] * 4,
+        out_specs=any_,
+        scratch_shapes=slab + [V(t.shape, bf16) for t in parity] + [
+            V((2 * groups, B, BLOCK), f32), V((2, R, B), bf16), V((2, R, B), bf16), V((2, 2, R, 256), f32), DMA((2,)), DMA((2,)), DMA((2, 2)),
+        ],
+        compiler_params=pltpu.CompilerParams(vmem_limit_bytes=48 * 2**20),
+    )(total.reshape(B, 2 * B), *blocks, *parity)
     return gradient, resist
 
 

time: 205 us -> 172 us (0.84)
  matrix products: 32.2 us -> 0 us
  Pallas kernels: 164 us -> 168 us
  other arithmetic: 3.12 us -> 0 us
    dot_general x5 -> x0, matrix products: 32.2 us -> none  [the longest x1 20 us: fast(): lax.dot_general(lax.optimization_barrier(delta), table, (((0,), (0,)), ((...]
    pallas_call x0 -> x1, Pallas kernels: none -> 14.3 us  [fast(): pl.pallas_call(final_kernel, out_shape=jax.ShapeDtypeStruct((R, N), f32),...]
    pallas_call x1, Pallas kernels: 164 us -> 154 us  [call(): pl.pallas_call(kernel, out_shape=outs, in_specs=specs, out_specs=jax.tree...]
    dynamic_slice x1 -> x0, local copies, waits for them, and re-layouts: 2.67 us -> none  [fast(): lax.dynamic_slice_in_dim(table, part * B + crossed(kq) * C, C, 0)]
where the time goes in v2:
time: 172 us; the launch traced here: 171 us
  Pallas kernels  168 us (98%)
  local copies, waits for them, and re-layouts  2.38 us (1%)
    pallas_call x1, Pallas kernels, call(): pl.pallas_call(kernel, out_shape=outs, in_specs=specs, out_specs=jax.tree...  154 us
    pallas_call x1, Pallas kernels, fast(): pl.pallas_call(final_kernel, out_shape=jax.ShapeDtypeStruct((R, N), f32),...  14.3 us

profile of v2, /device:TPU:1, one launch (start us, length us, event | category | flops | bytes accessed | tf_op | source)
XLA Modules:
  0.0 171.3 jit_solution(4463885474459040072)
XLA Ops:
  0.6 154.0 %shard_map.122 = (f32[2,2,2,2,2,16,1024]{6,5,4,3,2,1,0:T(8,128)}, f32[128,1024]{1,0:T(8,128)}) custom-call(bf16[512,4096]{1,0:T(8,128)(2,1)} %mask_hbm.1, f32[2,4,64,512]{3,2,1,0:T(8,128)} %kern_mine.1, s32[128,1024]{1,0:T(8,128)} %target_hbm.1, bf16[4,256,4096]{2,1,0:T(8,128)(2,1)} %constant.16.clone.bh_hbm, bf16[4,256,4096]{2,1,0:T(8,128)(2,1)} %constant.17.clone.bl_hbm, ...), custom_call_target="tpu_custom_call" | custom-call | tf_op jit(solution)/shard_map/pallas_call | solution.py:665
  154.6 0.0 copy-start
  154.6 1.6 copy-done
  156.2 0.0 copy-start.1
  156.2 14.3 %shard_map.123 = f32[512,4096]{1,0:T(8,128)} custom-call(f32[512,1024]{1,0:T(8,128)S(1)} %bitcast.1, bf16[4,256,4096]{2,1,0:T(8,128)(2,1)} %constant.16.clone.bh_hbm, bf16[4,256,4096]{2,1,0:T(8,128)(2,1)} %constant.17.clone.bl_hbm, bf16[2,512,2048]{2,1,0:T(8,128)(2,1)} %constant.18.clone.eh_hbm, bf16[2,512,2048]{2,1,0:T(8,128)(2,1)} %constant.19.clone.el_hbm), custom_call_target="tpu_custom_call" | custom-call | tf_op jit(solution)/shard_map/pallas_call | solution.py:769
  170.5 0.0 copy-done.1
  170.5 0.8 copy.14
Async XLA Ops:
  154.6 1.6 copy-start
  156.2 14.3 %copy-start.1 = (f32[128,1024]{1,0:T(8,128)S(1)}, f32[128,1024]{1,0:T(8,128)}, u32[]{:S(2)}) copy-start(f32[128,1024]{1,0:T(8,128)} %get-tuple-element.9) | copy-start | bytes 1572868

commit v3 on v2

--- a/solution.py
+++ b/solution.py
@@ -220,10 +220,9 @@
     points = np.arange(G)
     angle = (f[:, None] * points[None, :]) % G * (2 * np.pi / G)
     c, s = np.cos(angle), np.sin(angle)
-    order = np.arange(G).reshape(8, 2, 2, G // 32).transpose(1, 2, 0, 3).reshape(2, G // 2)
-    lift = np.stack([np.block([[c.T[o], -s.T[o]], [s.T[o], c.T[o]]]) for o in order])
-    W = G // STRIPS
-    image = np.stack([np.concatenate([c[:, j * W : j * W + W], s[:, j * W : j * W + W]], 1) for j in range(STRIPS)])
+    order = np.arange(G).reshape(8, 2, 2, GROUPS, 8).transpose(1, 3, 2, 0, 4).reshape(2, GROUPS, G // 2 // GROUPS)
+    lift = np.stack([[np.block([[c.T[o], -s.T[o]], [s.T[o], c.T[o]]]) for o in part] for part in order])
+    image = np.concatenate([t[:, i : i + w] for i, w in STRIPS for t in (c, s)], 1)
     return split_constant(lift) + split_constant(image)
 
 
@@ -241,10 +240,11 @@
 NT = ((1,), (1,))
 PARTS = 4
 BLOCK = 128
-STRIPS = 8
-STRIP_ORDERS = ("xylh", "ylxh", "lxyh", "xylh", "ylxh", "lxyh", "xylh", "ylxh")
-SUM_TIMES = (4, 7, 9, 11)
-SPREAD_TIMES = (13, 15, 18, 22)
+GROUPS = 4
+SUM_BEATS = (5, 8, 10, 12)
+SPREAD_BEATS = (14, 16, 19, 22)
+STRIPS = ((0, 384), (384, 384), (768, 256))
+STRIP_ORDERS = ("xylh", "ylxh", "lxyh")
 DIMS = "yhlx"
 ORDERS = ("xylh", "ylxh", "lxyh", "xylh")
 SPACE_ORDERS = ("xlh", "lxh", "xlh", "lxh")
@@ -269,16 +269,17 @@
 
 
 class Scatter:
-    def __init__(self, me, partner, src, bufs, dims, order, lanes, send, recv):
-        self.me, self.partner, self.refs, self.dims = me, partner, [src] + list(bufs), dims
+    def __init__(self, me, partner, src, bufs, dims, order, lanes, send, recv, base={}):
+        self.me, self.partner, self.refs, self.dims, self.base = me, partner, [src] + list(bufs), dims, base
         self.order, self.lanes, self.send, self.recv = order, lanes, send, recv
+
+    def place(self, t, fixed):
+        return index(without(self.dims, self.order[:t]), {**self.base, **fixed}, self.lanes)
 
     def copy(self, t):
         d = self.order[t]
-        left = without(self.dims, self.order[:t])
         return remote(
-            self.refs[t].at[index(left, {d: 1 - self.me[d]}, self.lanes)],
-            self.refs[t + 1].at[index(without(left, d), {}, self.lanes)],
+            self.refs[t].at[self.place(t, {d: 1 - self.me[d]})], self.refs[t + 1].at[self.place(t + 1, {})],
             self.send.at[t], self.recv.at[t], self.partner[d],
         )
 
@@ -288,9 +289,8 @@
     def finish(self, t):
         self.copy(t).wait_recv()
         d = self.order[t]
-        left = without(self.dims, self.order[:t])
-        own = self.refs[t][index(left, {d: self.me[d]}, self.lanes)]
-        there = index(without(left, d), {}, self.lanes)
+        own = self.refs[t][self.place(t, {d: self.me[d]})]
+        there = self.place(t + 1, {})
         self.refs[t + 1][there] = self.refs[t + 1][there] + own
 
     def drain(self):
@@ -299,12 +299,12 @@
 
 
 class Gather:
-    def __init__(self, me, partner, ref, dims, order, lanes, send, recv):
-        self.me, self.partner, self.ref, self.dims = me, partner, ref, dims
+    def __init__(self, me, partner, ref, dims, order, lanes, send, recv, base={}):
+        self.me, self.partner, self.ref, self.dims, self.base = me, partner, ref, dims, base
         self.order, self.lanes, self.send, self.recv = order, lanes, send, recv
 
     def copy(self, t, theirs):
-        fixed = {d: self.me[d] for d in self.order[t:]}
+        fixed = {**self.base, **{d: self.me[d] for d in self.order[t:]}}
         if theirs:
             fixed[self.order[t]] = 1 - fixed[self.order[t]]
         view = self.ref.at[index(self.dims, fixed, self.lanes)]
@@ -325,11 +325,11 @@
     mask_hbm, kern_mine, target_hbm, bh_hbm, bl_hbm, lh_hbm, ll_hbm, th_hbm, tl_hbm,
     out_ref, resist_ref,
     lh, ll, th, tl, table_sem, mbuf, fh, fl, load_sem, slabh, slabl, target_ref, slab_sem, columns, part_ref,
-    kbuf, p0, p1, p2, spec, ph, pw, cout, cin, ch, cl, field,
+    kbuf, p0, p1, p2, spec, ph, pw, cout, cin, ch, cl, field, mh, ml,
     light, l0, l1, l2, l3, slope, grad, gin, acc, sums, s0, s1, s2, s3,
     ks, kr_, ps, pr_, as_, ar, xs, xr, ls, lr, gs, gr, cs, cr, ss, sr_, os_, or_, fs, fr, us, ur,
 ):
-    H, W, C = G // 2, G // STRIPS, B // 2
+    H, C = G // 2 // GROUPS, B // 2
     sp, kq = lax.axis_index("space"), lax.axis_index("kern")
     z, x = sp // 2, lax.rem(sp, 2)
     y, core = kq // 2, lax.rem(kq, 2)
@@ -342,7 +342,7 @@
     }
     sibling = (sp, y * 2 + 1 - core)
     lanes = [pl.ds(j * (2 * B // PARTS), 2 * B // PARTS) for j in range(PARTS)]
-    strips = [pl.ds(j * W, W) for j in range(STRIPS)]
+    strips = [pl.ds(i, w) for i, w in STRIPS]
     span = N // 4
     loads = []
     for i in range(4):
@@ -368,14 +368,16 @@
     for device in list(partner.values()) + [sibling]:
         pl.semaphore_signal(barrier, inc=1, device_id=device, device_id_type=MESH)
     half, slot = sp // 4, lax.rem(sp, 4)
-    holder = [(core * 4 + k, y * 2 + half) for k in range(4)]
-    stays = [jnp.logical_and(half == core, slot == k) for k in range(4)]
-    for k in range(4):
-        @pl.when(jnp.logical_not(stays[k]))
+    stays = jnp.logical_and(half == core, x == core)
+    kinds = [lax.rem(2 * (1 - half) + i, 4) for i in range(4)]
+    leaves = [jnp.logical_not(jnp.logical_and(stays, k == z)) for k in kinds]
+    comes = [jnp.logical_not(jnp.logical_and(stays, slot == i)) for i in range(4)]
+    for i in range(4):
+        @pl.when(comes[i])
         def _():
-            pl.semaphore_signal(barrier, inc=1, device_id=holder[k], device_id_type=MESH)
-
-    pl.semaphore_wait(barrier, 9 - jnp.where(half == core, 1, 0))
+            pl.semaphore_signal(barrier, inc=1, device_id=(core * 4 + i, y * 2 + x), device_id_type=MESH)
+
+    pl.semaphore_wait(barrier, 9 - jnp.where(stays, 1, 0))
 
     scatter = [
         Scatter(me, partner, part_ref, (p0, p1, p2), "hlx", SPACE_ORDERS[j], lanes[j], ps.at[j], pr_.at[j])
@@ -384,24 +386,26 @@
     gather = [
         Gather(me, partner, spec, DIMS, ORDERS[j][::-1], lanes[j], as_.at[j], ar.at[j]) for j in range(PARTS)
     ]
-    def kern_copy(k, place):
-        return remote(kern_mine.at[:, k], kbuf.at[:, place], ks.at[k], kr_.at[place], holder[k])
-
-    def kern_stay(k):
-        return pltpu.make_async_copy(kern_mine.at[:, k], kbuf.at[:, k], kr_.at[k])
-
-    def kern_send(k):
-        @pl.when(jnp.logical_not(stays[k]))
+    def kern_copy(i, place):
+        k = kinds[i]
+        return remote(
+            kern_mine.at[:, k], kbuf.at[:, place], ks.at[i], kr_.at[place], (2 * k + core, y * 2 + half)
+        )
+
+    def kern_stay():
+        return pltpu.make_async_copy(kern_mine.at[:, z], kbuf.at[:, slot], kr_.at[slot])
+
+    def kern_send(i):
+        @pl.when(leaves[i])
         def _():
-            kern_copy(k, slot).start()
-
-        @pl.when(stays[k])
-        def _():
-            kern_stay(k).start()
-
-    kern_send(0)
-    kern_send(1)
-
+            kern_copy(i, slot).start()
+
+    @pl.when(stays)
+    def _():
+        kern_stay().start()
+
+    for i in range(4):
+        kern_send(i)
     for i in range(4):
         for t in loads[i]:
             t.wait()
@@ -422,7 +426,6 @@
                 value = value[:BLOCK, BLOCK:] + value[BLOCK:, :BLOCK]
             part_ref[:, :, :, :, pl.ds((2 * j + i) * BLOCK, BLOCK)] = value.reshape(2, 2, 2, 16, BLOCK)
         scatter[j].start(0)
-    kern_send(2)
 
     for t in range(3):
         for s in scatter:
@@ -432,20 +435,19 @@
     for j in range(PARTS):
         spec[index(DIMS, me, lanes[j])] = p2[:, lanes[j]]
         gather[j].start(0)
-    kern_send(3)
     for t in range(4):
         for g in gather:
             g.finish(t)
             if t < 3:
                 g.start(t + 1)
-    for k in range(4):
-        @pl.when(jnp.logical_not(stays[k]))
+    for i in range(4):
+        @pl.when(comes[i])
         def _():
-            kern_copy(k, k).wait_recv()
-
-        @pl.when(stays[k])
-        def _():
-            kern_stay(k).wait()
+            kern_copy(0, i).wait_recv()
+
+    @pl.when(stays)
+    def _():
+        kern_stay().wait()
 
     def product(i, c):
         rows = pl.ds(pl.multiple_of(i * 64, 64), 64)
@@ -457,124 +459,156 @@
         return c
 
     lax.fori_loop(0, 4, product, 0)
-    tables[0].wait()
-    tables[1].wait()
-
-    def lift(d, i):
-        rows = pl.ds(pl.multiple_of(i * 256, 256), 256)
-        return dot3(lh[d, rows, :], ll[d, rows, :], ph[...], pw[...], NT)
-
-    def cross_copy(i):
-        return remote(cout.at[i], cin.at[i], xs.at[i], xr.at[i], sibling)
-
-    def lift_other(i, c):
-        cout[i] = lift(1 - core, i)
-        cross_copy(i).start()
+
+    mine = pl.ds(pl.multiple_of(core * C, C), C)
+    other = pl.ds(pl.multiple_of((1 - core) * C, C), C)
+
+    def lift(d, g):
+        return dot3(lh[d, g], ll[d, g], ph[...], pw[...], NT)
+
+    def cross_copy(g):
+        return remote(cout.at[g], cin.at[g], xs.at[g], xr.at[g], sibling)
+
+    def lift_other(g):
+        cout[g] = lift(1 - core, g)
+        cross_copy(g).start()
+
+    def lift_own(g):
+        ch[g, :, mine], cl[g, :, mine] = halves(lift(core, g))
+
+    def cross_land(g):
+        cross_copy(g).wait_recv()
+        ch[g, :, other], cl[g, :, other] = halves(cin[g])
+
+    def add_light(g):
+        return [
+            Scatter(
+                me, partner, light, (l0, l1, l2, l3), "g" + DIMS, o, strips[i], ls.at[g, i], lr.at[g, i], {"g": g}
+            )
+            for i, o in enumerate(STRIP_ORDERS)
+        ]
+
+    def spread(g):
+        return [
+            Gather(me, partner, slope, "g" + DIMS, o[::-1], strips[i], gs.at[g, i], gr.at[g, i], {"g": g})
+            for i, o in enumerate(STRIP_ORDERS)
+        ]
+
+    def image(g, i):
+        start, w = STRIPS[i]
+        cols = pl.ds(2 * start, 2 * w)
+        value = dot3(ch[g], cl[g], th[:, cols], tl[:, cols], NN)
+        re = value[:H, :w] - value[H:, w:]
+        im = value[:H, w:] + value[H:, :w]
+        field[g, :H, strips[i]] = re
+        field[g, H:, strips[i]] = im
+        light[g, :, :, :, :, :, strips[i]] = (re * re + im * im).reshape(2, 2, 2, 2, 8, w)
+
+    def expose(g, i):
+        rows = pl.ds(pl.multiple_of(core * 64 + y * 32 + g * 8, 8), 8)
+        intensity = l3[g, :, strips[i]] * (1.0 / (B * B))
+        resist = jax.nn.sigmoid(steepness * (intensity - threshold))
+        resist_ref[rows, strips[i]] = resist
+        goal = target_ref[rows, strips[i]].astype(jnp.float32)
+        slope[index("g" + DIMS, {**me, "g": g}, strips[i])] = (
+            (4.0 * steepness / (B * B)) * (resist - goal) * resist * (1.0 - resist)
+        )
+
+    def back(g):
+        for i, (start, w) in enumerate(STRIPS):
+            scale = slope[g, :, :, :, :, :, strips[i]].reshape(H, w)
+            rh, rl = halves(field[g, :H, strips[i]] * scale)
+            ih, il = halves(field[g, H:, strips[i]] * scale)
+            one, two = pl.ds(2 * start, w), pl.ds(2 * start + w, w)
+            mh[:H, one], mh[:H, two], mh[H:, one], mh[H:, two] = rh, ih, ih, -rh
+            ml[:H, one], ml[:H, two], ml[H:, one], ml[H:, two] = rl, il, il, -rl
+
+    def back_rows(g, rows):
+        grad[g, rows, :] = dot3(th[rows, :], tl[rows, :], mh[...], ml[...], NT)
+
+    def grad_copy(g):
+        return remote(grad.at[g, other], gin.at[g], cs.at[g], cr.at[g], sibling)
+
+    def adjoint(value, d, g):
+        dh, dl = halves(value)
+        return dot3(dh, dl, lh[d, g], ll[d, g], NN)
+
+    def adjoint_own(g):
+        acc[...] = acc[...] + adjoint(grad[g, mine, :], core, g)
+
+    def adjoint_land(g):
+        grad_copy(g).wait_recv()
+        acc[...] = acc[...] + adjoint(gin[g], 1 - core, g)
+
+    def show(g, i):
+        if i == 0:
+            lift_own(g)
+
+            @pl.when(g < GROUPS - 1)
+            def _():
+                lift_other(g + 1)
+
+            cross_land(g)
+        image(g, i)
+        add_light(g)[i].start(0)
+
+    def add_step(n, g, i):
+        s = add_light(g)[i]
+        s.finish(n)
+        if n < 3:
+            s.start(n + 1)
+        else:
+            expose(g, i)
+            spread(g)[i].start(0)
+
+    def spread_step(n, g, i):
+        s = spread(g)[i]
+        s.finish(n)
+        if n < 3:
+            s.start(n + 1)
+
+    def back_first(g, i):
+        back(g)
+        back_rows(g, other)
+        grad_copy(g).start()
+
+    def back_second(g, i):
+        back_rows(g, mine)
+
+    def back_third(g, i):
+        adjoint_own(g)
+
+        @pl.when(g > 0)
+        def _():
+            adjoint_land(g - 1)
+
+    items = []
+    stages = [(0, 1, show)]
+    stages += [(SUM_BEATS[n], 2, functools.partial(add_step, n)) for n in range(4)]
+    stages += [(SPREAD_BEATS[n], -1 if n == 3 else 0, functools.partial(spread_step, n)) for n in range(4)]
+    last = SPREAD_BEATS[3] + 2
+    stages += [(last, 0, back_first), (last + 1, 0, back_second), (last + 2, 0, back_third)]
+    for beat, rank, body in stages:
+        for i in range(len(STRIPS) if beat < last else 1):
+            items.append(((beat + i) % len(STRIPS), rank, -beat, (beat + i) // len(STRIPS), i, body))
+    items.sort(key=lambda e: e[:3])
+    ticks = GROUPS + max(e[3] for e in items)
+
+    def tick(t, c):
+        for _, _, _, late, i, body in items:
+            g = t - late
+
+            @pl.when(jnp.logical_and(g >= 0, g < GROUPS))
+            def _():
+                body(g, i)
+
         return c
 
-    lax.fori_loop(0, 4, lift_other, 0)
-
-    def lift_own(i, c):
-        rows = pl.ds(pl.multiple_of(i * 256, 256), 256)
-        mine = pl.ds(pl.multiple_of(core * C, C), C)
-        ch[rows, mine], cl[rows, mine] = halves(lift(core, i))
-        return c
-
-    lax.fori_loop(0, 4, lift_own, 0)
-
-    def cross_land(i, c):
-        rows = pl.ds(pl.multiple_of(i * 256, 256), 256)
-        other = pl.ds(pl.multiple_of((1 - core) * C, C), C)
-        cross_copy(i).wait_recv()
-        ch[rows, other], cl[rows, other] = halves(cin[i])
-        return c
-
-    lax.fori_loop(0, 4, cross_land, 0)
-    tables[2].wait()
-    tables[3].wait()
-
-    add_light = [
-        Scatter(me, partner, light, (l0, l1, l2, l3), DIMS, STRIP_ORDERS[j], strips[j], ls.at[j], lr.at[j])
-        for j in range(STRIPS)
-    ]
-    spread = [
-        Gather(me, partner, slope, DIMS, STRIP_ORDERS[j][::-1], strips[j], gs.at[j], gr.at[j]) for j in range(STRIPS)
-    ]
-    own_rows = pl.ds(pl.multiple_of(core * 64 + y * 32, 32), 32)
-
-    def image(j):
-        def chunk(i, c):
-            top = pl.ds(pl.multiple_of(i * 256, 256), 256)
-            low = pl.ds(pl.multiple_of(H + i * 256, 256), 256)
-            a = dot3(ch[top, :], cl[top, :], th[j], tl[j], NN)
-            b = dot3(ch[low, :], cl[low, :], th[j], tl[j], NN)
-            re = a[:, :W] - b[:, W:]
-            im = a[:, W:] + b[:, :W]
-            field[top, strips[j]] = re
-            field[low, strips[j]] = im
-            light[i, :, :, :, :, strips[j]] = (re * re + im * im).reshape(2, 2, 2, 32, W)
-            return c
-
-        lax.fori_loop(0, 2, chunk, 0)
-
-    def expose(j):
-        intensity = l3[:, strips[j]] * (1.0 / (B * B))
-        resist = jax.nn.sigmoid(steepness * (intensity - threshold))
-        resist_ref[own_rows, strips[j]] = resist
-        goal = target_ref[own_rows, strips[j]].astype(jnp.float32)
-        slope[index(DIMS, me, strips[j])] = (4.0 * steepness / (B * B)) * (resist - goal) * resist * (1.0 - resist)
-
-    def back(j):
-        def chunk(i, c):
-            top = pl.ds(pl.multiple_of(i * 256, 256), 256)
-            low = pl.ds(pl.multiple_of(H + i * 256, 256), 256)
-            scale = slope[i, :, :, :, :, strips[j]].reshape(256, W)
-            rh, rl = halves(field[top, strips[j]] * scale)
-            ih, il = halves(field[low, strips[j]] * scale)
-            one = dot3(
-                th[j], tl[j], jnp.concatenate([rh, ih], 1), jnp.concatenate([rl, il], 1), NT
-            )
-            two = dot3(
-                th[j], tl[j], jnp.concatenate([ih, -rh], 1), jnp.concatenate([il, -rl], 1), NT
-            )
-            if j == 0:
-                grad[:, top] = one
-                grad[:, low] = two
-            else:
-                grad[:, top] = grad[:, top] + one
-                grad[:, low] = grad[:, low] + two
-            return c
-
-        lax.fori_loop(0, 2, chunk, 0)
-
-    def show(j):
-        image(j)
-        add_light[j].start(0)
-
-    def add_step(j, t):
-        add_light[j].finish(t)
-        if t < 3:
-            add_light[j].start(t + 1)
-        else:
-            expose(j)
-            spread[j].start(0)
-
-    def spread_step(j, t):
-        spread[j].finish(t)
-        if t < 3:
-            spread[j].start(t + 1)
-        else:
-            back(j)
-
-    events = []
-    for j in range(STRIPS):
-        events.append((j, 0, j, functools.partial(show, j)))
-        for t in range(4):
-            events.append((j + SUM_TIMES[t], 2, j, functools.partial(add_step, j, t)))
-            events.append((j + SPREAD_TIMES[t], 3 if t == 3 else 1, j, functools.partial(spread_step, j, t)))
-    others[2].wait()
-    for event in sorted(events, key=lambda e: e[:3]):
-        event[3]()
+    for t in tables + others[2:]:
+        t.wait()
+    acc[...] = jnp.zeros_like(acc)
+    lift_other(0)
+    lax.fori_loop(0, ticks, tick, 0)
 
     def resist_copy(i, rows, device):
         return remote(resist_ref.at[rows], resist_ref.at[rows], us.at[i], ur.at[i], device)
@@ -583,28 +617,16 @@
     resist_copy(0, row_of(core, y), partner["y"]).start()
     resist_copy(1, row_of(core, y), sibling).start()
 
-    def grad_copy():
-        rows = pl.ds(pl.multiple_of((1 - core) * C, C), C)
-        return remote(grad.at[rows], gin, cs, cr, sibling)
-
-    grad_copy().start()
-
-    def adjoint(dh, dl, d, cols):
-        return dot3(dh, dl, lh[d, :, cols], ll[d, :, cols], NN)
-
-    gh, gl = halves(grad[pl.ds(pl.multiple_of(core * C, C), C), :])
-    for cols in lanes:
-        acc[:, cols] = adjoint(gh, gl, core, cols)
-    grad_copy().wait_recv()
-    gh, gl = halves(gin[...])
+    grad_copy(GROUPS - 1).wait_recv()
+    gh, gl = halves(gin[GROUPS - 1])
+    far = lambda cols: dot3(gh, gl, lh[1 - core, GROUPS - 1, :, cols], ll[1 - core, GROUPS - 1, :, cols], NN)
     add_sums = [
         Scatter(me, partner, sums, (s0, s1, s2, s3), DIMS, ORDERS[j], lanes[j], ss.at[j], sr_.at[j])
         for j in range(PARTS)
     ]
     for j in range(2):
-        cols = lanes[j]
-        pr = acc[:, lanes[j]] + adjoint(gh, gl, 1 - core, lanes[j])
-        pi = acc[:, lanes[j + 2]] + adjoint(gh, gl, 1 - core, lanes[j + 2])
+        pr = acc[:, lanes[j]] + far(lanes[j])
+        pi = acc[:, lanes[j + 2]] + far(lanes[j + 2])
         kr = kbuf[0, :, :, lanes[j]].reshape(C, C)
         ki = kbuf[1, :, :, lanes[j]].reshape(C, C)
         sums[:, :, :, :, :, lanes[j]] = (kr * pr + ki * pi).reshape(2, 2, 2, 2, 16, C)
@@ -644,17 +666,23 @@
 
     for j in range(PARTS):
         final_copy(j, core).wait_send()
-    for group in (scatter, gather, add_light, spread, add_sums, deliver):
+    for group in (scatter, gather, add_sums, deliver):
         for one in group:
             one.drain()
-    for k in range(4):
-        @pl.when(jnp.logical_not(stays[k]))
+
+    def drain(g, c):
+        for one in add_light(g) + spread(g):
+            one.drain()
+        cross_copy(g).wait_send()
+        grad_copy(g).wait_send()
+        return c
+
+    lax.fori_loop(0, GROUPS, drain, 0)
+    for i in range(4):
+        @pl.when(leaves[i])
         def _():
-            kern_copy(k, slot).wait_send()
-
-    for i in range(4):
-        cross_copy(i).wait_send()
-    grad_copy().wait_send()
+            kern_copy(i, slot).wait_send()
+
     resist_copy(0, row_of(core, y), partner["y"]).wait_send()
     resist_copy(1, row_of(core, y), sibling).wait_send()
     resist_copy(2, row_of(core, 1 - y), sibling).wait_send()
@@ -753,15 +781,17 @@
             V(two + (16, 2 * B), f32),
             V((B // 2, 2 * B), bf16), V((B // 2, 2 * B), bf16),
             V((4, 256, B // 2), f32), V((4, 256, B // 2), f32),
-            V((G, B), bf16), V((G, B), bf16), V((G, G), f32),
-            V(two + (32, G), f32), V((2, 2, 2, 32, G), f32), V((2, 2, 32, G), f32), V((2, 32, G), f32), V((32, G), f32),
-            V(two + (32, G), f32),
-            V((B, G), f32), V((B // 2, G), f32), V((B // 2, 2 * B), f32),
+            V((GROUPS, G // GROUPS, B), bf16), V((GROUPS, G // GROUPS, B), bf16), V((GROUPS, G // GROUPS, G), f32),
+            V((G // GROUPS, 2 * G), bf16), V((G // GROUPS, 2 * G), bf16),
+            V((GROUPS,) + two + (8, G), f32), V((GROUPS, 2, 2, 2, 8, G), f32), V((GROUPS, 2, 2, 8, G), f32),
+            V((GROUPS, 2, 8, G), f32), V((GROUPS, 8, G), f32),
+            V((GROUPS,) + two + (8, G), f32),
+            V((GROUPS, B, G // GROUPS), f32), V((GROUPS, B // 2, G // GROUPS), f32), V((B // 2, 2 * B), f32),
             V(two + (16, 2 * B), f32), V((2, 2, 2, 16, 2 * B), f32), V((2, 2, 16, 2 * B), f32), V((2, 16, 2 * B), f32),
             V((16, 2 * B), f32),
             DMA((4,)), DMA((4,)), DMA((PARTS, 3)), DMA((PARTS, 3)), DMA((PARTS, 4)), DMA((PARTS, 4)),
-            DMA((4,)), DMA((4,)), DMA((STRIPS, 4)), DMA((STRIPS, 4)), DMA((STRIPS, 4)), DMA((STRIPS, 4)),
-            DMA, DMA, DMA((PARTS, 4)), DMA((PARTS, 4)), DMA((PARTS, 4)), DMA((PARTS, 4)),
+            DMA((4,)), DMA((4,))] + [DMA((GROUPS, len(STRIPS), 4))] * 4 + [
+            DMA((GROUPS,)), DMA((GROUPS,)), DMA((PARTS, 4)), DMA((PARTS, 4)), DMA((PARTS, 4)), DMA((PARTS, 4)),
             DMA((PARTS,)), DMA((PARTS,)), DMA((3,)), DMA((3,)),
         ],
         1, (mask, kernels, target) + blocks + consts, 59,

time: 172 us -> 164 us (0.953)
  Pallas kernels: 168 us -> 161 us
    pallas_call x1, Pallas kernels: 154 us -> 146 us  [call(): pl.pallas_call(kernel, out_shape=outs, in_specs=specs, out_specs=jax.tree...]
where the time goes in v3:
time: 164 us
  Pallas kernels  161 us (98%)
  local copies, waits for them, and re-layouts  2.38 us (1%)
    pallas_call x1, Pallas kernels, call(): pl.pallas_call(kernel, out_shape=outs, in_specs=specs, out_specs=jax.tree...  146 us
    pallas_call x1, Pallas kernels, fast(): pl.pallas_call(final_kernel, out_shape=jax.ShapeDtypeStruct((R, N), f32),...  14.3 us

profile of v3, /device:TPU:1, one launch (start us, length us, event | category | flops | bytes accessed | tf_op | source)
XLA Modules:
  0.0 163.7 jit_solution(65501751058647776)
XLA Ops:
  0.6 146.3 %shard_map.122 = (f32[2,2,2,2,2,16,1024]{6,5,4,3,2,1,0:T(8,128)}, f32[128,1024]{1,0:T(8,128)}) custom-call(bf16[512,4096]{1,0:T(8,128)(2,1)} %mask_hbm.1, f32[2,4,64,512]{3,2,1,0:T(8,128)} %kern_mine.1, s32[128,1024]{1,0:T(8,128)} %target_hbm.1, bf16[4,256,4096]{2,1,0:T(8,128)(2,1)} %constant.16.clone.bh_hbm, bf16[4,256,4096]{2,1,0:T(8,128)(2,1)} %constant.17.clone.bl_hbm, ...), custom_call_target="tpu_custom_call" | custom-call | tf_op jit(solution)/shard_map/pallas_call | solution.py:693
  146.9 0.0 copy-start
  146.9 1.6 copy-done
  148.5 0.0 copy-start.1
  148.5 14.3 %shard_map.123 = f32[512,4096]{1,0:T(8,128)} custom-call(f32[512,1024]{1,0:T(8,128)S(1)} %bitcast.1, bf16[4,256,4096]{2,1,0:T(8,128)(2,1)} %constant.16.clone.bh_hbm, bf16[4,256,4096]{2,1,0:T(8,128)(2,1)} %constant.17.clone.bl_hbm, bf16[2,512,2048]{2,1,0:T(8,128)(2,1)} %constant.18.clone.eh_hbm, bf16[2,512,2048]{2,1,0:T(8,128)(2,1)} %constant.19.clone.el_hbm), custom_call_target="tpu_custom_call" | custom-call | tf_op jit(solution)/shard_map/pallas_call | solution.py:799
  162.9 0.0 copy-done.1
  162.9 0.8 copy.14
Async XLA Ops:
  146.9 1.6 copy-start
  148.5 14.3 %copy-start.1 = (f32[128,1024]{1,0:T(8,128)S(1)}, f32[128,1024]{1,0:T(8,128)}, u32[]{:S(2)}) copy-start(f32[128,1024]{1,0:T(8,128)} %get-tuple-element.9) | copy-start | bytes 1572868

commit v4 on v3

--- a/solution.py
+++ b/solution.py
@@ -233,7 +233,8 @@
 
 def dot3(ah, al, bh, bl, dims):
     d = functools.partial(lax.dot_general, dimension_numbers=(dims, ((), ())), preferred_element_type=jnp.float32)
-    return d(ah, bh) + (d(al, bh) + d(ah, bl))
+    both, rows = d(jnp.concatenate([ah, al], axis=0), bh), ah.shape[0]
+    return both[:rows] + (both[rows:] + d(ah, bl))
 
 
 NN = ((1,), (0,))
@@ -246,7 +247,7 @@
 STRIPS = ((0, 384), (384, 384), (768, 256))
 STRIP_ORDERS = ("xylh", "ylxh", "lxyh")
 DIMS = "yhlx"
-ORDERS = ("xylh", "ylxh", "lxyh", "xylh")
+PLANE_ORDERS = ("xy", "yx", "xy", "yx")
 SPACE_ORDERS = ("xlh", "lxh", "xlh", "lxh")
 
 
@@ -326,8 +327,8 @@
     out_ref, resist_ref,
     lh, ll, th, tl, table_sem, mbuf, fh, fl, load_sem, slabh, slabl, target_ref, slab_sem, columns, part_ref,
     kbuf, p0, p1, p2, spec, ph, pw, cout, cin, ch, cl, field, mh, ml,
-    light, l0, l1, l2, l3, slope, grad, gin, acc, sums, s0, s1, s2, s3,
-    ks, kr_, ps, pr_, as_, ar, xs, xr, ls, lr, gs, gr, cs, cr, ss, sr_, os_, or_, fs, fr, us, ur,
+    light, l0, l1, l2, l3, slope, grad, gin, acc, sums, s0, s1, s2,
+    ks, kr_, ps, pr_, as_, ar, xs, xr, ls, lr, gs, gr, cs, cr, ss, sr_, os_, or_, fs, fr, us, ur, zs, zr,
 ):
     H, C = G // 2 // GROUPS, B // 2
     sp, kq = lax.axis_index("space"), lax.axis_index("kern")
@@ -344,12 +345,13 @@
     lanes = [pl.ds(j * (2 * B // PARTS), 2 * B // PARTS) for j in range(PARTS)]
     strips = [pl.ds(i, w) for i, w in STRIPS]
     span = N // 4
-    loads = []
-    for i in range(4):
-        cols = pl.ds(i * span, span)
+
+    def loads(i):
+        cols = pl.ds(pl.multiple_of(i * span, span), span)
         blk = 2 * core + y
         pairs = [(mask_hbm.at[:, cols], mbuf.at[i]), (bh_hbm.at[blk, :, cols], fh.at[i]), (bl_hbm.at[blk, :, cols], fl.at[i])]
-        loads.append([pltpu.make_async_copy(a, b, load_sem.at[i, n]) for n, (a, b) in enumerate(pairs)])
+        return [pltpu.make_async_copy(a, b, load_sem.at[i, n]) for n, (a, b) in enumerate(pairs)]
+
     rows_mine = pl.ds(pl.multiple_of(sp * (N // 8), N // 8), N // 8)
     others = [
         pltpu.make_async_copy(a, b, slab_sem.at[n])
@@ -361,11 +363,26 @@
         pltpu.make_async_copy(src, dst, table_sem.at[i])
         for i, (src, dst) in enumerate(zip((lh_hbm, ll_hbm, th_hbm, tl_hbm), (lh, ll, th, tl)))
     ]
-    for t in sum(loads, []) + others + tables:
+    for t in sum([loads(i) for i in range(4)], []) + others:
         t.start()
 
+    far_z = [lax.rem(z + o, 4) for o in range(1, 4)]
+
+    def z_copy(use, j, src, dst, to, slot):
+        return remote(src, dst, zs.at[use, j, to], zr.at[use, j, slot], (to * 2 + x, kq))
+
+    def z_block(ref, j, zz):
+        return ref.at[index(DIMS, {"y": y, "x": x, "h": zz // 2, "l": lax.rem(zz, 2)}, lanes[j])]
+
+    def z_spread(use, ref, j):
+        return [z_copy(use, j, z_block(ref, j, z), z_block(ref, j, z), zz, z) for zz in far_z]
+
+    def z_spread_land(use, ref, j):
+        for zz in far_z:
+            z_copy(use, j, z_block(ref, j, zz), z_block(ref, j, zz), zz, zz).wait_recv()
+
     barrier = pltpu.get_barrier_semaphore()
-    for device in list(partner.values()) + [sibling]:
+    for device in list(partner.values()) + [sibling, ((3 - z) * 2 + x, kq)]:
         pl.semaphore_signal(barrier, inc=1, device_id=device, device_id_type=MESH)
     half, slot = sp // 4, lax.rem(sp, 4)
     stays = jnp.logical_and(half == core, x == core)
@@ -377,14 +394,14 @@
         def _():
             pl.semaphore_signal(barrier, inc=1, device_id=(core * 4 + i, y * 2 + x), device_id_type=MESH)
 
-    pl.semaphore_wait(barrier, 9 - jnp.where(stays, 1, 0))
+    pl.semaphore_wait(barrier, 10 - jnp.where(stays, 1, 0))
 
     scatter = [
         Scatter(me, partner, part_ref, (p0, p1, p2), "hlx", SPACE_ORDERS[j], lanes[j], ps.at[j], pr_.at[j])
         for j in range(PARTS)
     ]
     gather = [
-        Gather(me, partner, spec, DIMS, ORDERS[j][::-1], lanes[j], as_.at[j], ar.at[j]) for j in range(PARTS)
+        Gather(me, partner, spec, DIMS, PLANE_ORDERS[j][::-1], lanes[j], as_.at[j], ar.at[j]) for j in range(PARTS)
     ]
     def kern_copy(i, place):
         k = kinds[i]
@@ -406,26 +423,36 @@
 
     for i in range(4):
         kern_send(i)
-    for i in range(4):
-        for t in loads[i]:
+    columns[...] = jnp.zeros_like(columns)
+
+    def sweep(i, c):
+        for t in loads(i):
             t.wait()
         m = mbuf[i]
         d = functools.partial(lax.dot_general, dimension_numbers=(NT, ((), ())), preferred_element_type=jnp.float32)
-        piece = d(fh[i], m) + d(fl[i], m)
-        columns[...] = piece if i == 0 else columns[...] + piece
+        both = d(jnp.concatenate([fh[i], fl[i]], axis=0), m)
+        columns[...] += both[: 2 * BLOCK] + both[2 * BLOCK :]
+        return c
+
+    lax.fori_loop(0, 4, sweep, 0)
+    for t in tables:
+        t.start()
     for t in others[:2]:
         t.wait()
     colh, coll = halves(columns[...] * (1.0 / N))
-    for j in range(PARTS):
-        for i in range(2):
-            n = j % 2 * 2 + i
-            value = dot3(colh, coll, slabh[n], slabl[n], NT)
-            if j < 2:
-                value = value[:BLOCK, :BLOCK] - value[BLOCK:, BLOCK:]
-            else:
-                value = value[:BLOCK, BLOCK:] + value[BLOCK:, :BLOCK]
-            part_ref[:, :, :, :, pl.ds((2 * j + i) * BLOCK, BLOCK)] = value.reshape(2, 2, 2, 16, BLOCK)
-        scatter[j].start(0)
+
+    def band(n, c):
+        value = dot3(colh, coll, slabh[n], slabl[n], NT)
+        re = value[:BLOCK, :BLOCK] - value[BLOCK:, BLOCK:]
+        im = value[:BLOCK, BLOCK:] + value[BLOCK:, :BLOCK]
+        at = pl.multiple_of(n * BLOCK, BLOCK)
+        part_ref[:, :, :, :, pl.ds(at, BLOCK)] = re.reshape(2, 2, 2, 16, BLOCK)
+        part_ref[:, :, :, :, pl.ds(B + at, BLOCK)] = im.reshape(2, 2, 2, 16, BLOCK)
+        return c
+
+    lax.fori_loop(0, B // BLOCK, band, 0)
+    for one in scatter:
+        one.start(0)
 
     for t in range(3):
         for s in scatter:
@@ -434,11 +461,15 @@
                 s.start(t + 1)
     for j in range(PARTS):
         spec[index(DIMS, me, lanes[j])] = p2[:, lanes[j]]
-        gather[j].start(0)
-    for t in range(4):
+        for one in z_spread(0, spec, j):
+            one.start()
+    for j, g in enumerate(gather):
+        z_spread_land(0, spec, j)
+        g.start(0)
+    for t in range(2):
         for g in gather:
             g.finish(t)
-            if t < 3:
+            if t < 1:
                 g.start(t + 1)
     for i in range(4):
         @pl.when(comes[i])
@@ -621,7 +652,7 @@
     gh, gl = halves(gin[GROUPS - 1])
     far = lambda cols: dot3(gh, gl, lh[1 - core, GROUPS - 1, :, cols], ll[1 - core, GROUPS - 1, :, cols], NN)
     add_sums = [
-        Scatter(me, partner, sums, (s0, s1, s2, s3), DIMS, ORDERS[j], lanes[j], ss.at[j], sr_.at[j])
+        Scatter(me, partner, sums, (s0, s1), DIMS, PLANE_ORDERS[j], lanes[j], ss.at[j], sr_.at[j])
         for j in range(PARTS)
     ]
     for j in range(2):
@@ -635,25 +666,43 @@
         add_sums[j + 2].start(0)
     out_mine = out_ref.at[core]
     deliver = [
-        Gather(me, partner, out_mine, DIMS, ORDERS[j][::-1], lanes[j], os_.at[j], or_.at[j]) for j in range(PARTS)
+        Gather(me, partner, out_mine, DIMS, PLANE_ORDERS[j][::-1], lanes[j], os_.at[j], or_.at[j])
+        for j in range(PARTS)
     ]
-    for t in range(4):
-        for j, s in enumerate(add_sums):
-            s.finish(t)
-            if t < 3:
-                s.start(t + 1)
-            else:
-                out_ref[(core,) + index(DIMS, me, lanes[j])] = s3[:, lanes[j]]
-                deliver[j].start(0)
+
+    def part_of(j, zz):
+        return s1.at[zz // 2, lax.rem(zz, 2), :, lanes[j]]
+
+    def z_send(j, zz):
+        return z_copy(1, j, part_of(j, zz), s2.at[z, :, lanes[j]], zz, z)
+
+    for j, s in enumerate(add_sums):
+        s.finish(0)
+        s.start(1)
+    for j, s in enumerate(add_sums):
+        s.finish(1)
+        for zz in far_z:
+            z_send(j, zz).start()
+    for j in range(PARTS):
+        value = s1[me["h"], me["l"], :, lanes[j]]
+        for zz in far_z:
+            z_copy(1, j, part_of(j, zz), s2.at[zz, :, lanes[j]], zz, zz).wait_recv()
+            value = value + s2[zz, :, lanes[j]]
+        out_ref[(core,) + index(DIMS, me, lanes[j])] = value
+        for one in z_spread(2, out_mine, j):
+            one.start()
 
     def final_copy(j, c):
         view = out_ref.at[(c,) + index(DIMS, {}, lanes[j])]
         return remote(view, view, fs.at[j], fr.at[j], sibling)
 
-    for t in range(4):
+    for j, g in enumerate(deliver):
+        z_spread_land(2, out_mine, j)
+        g.start(0)
+    for t in range(2):
         for j, g in enumerate(deliver):
             g.finish(t)
-            if t < 3:
+            if t < 1:
                 g.start(t + 1)
             else:
                 final_copy(j, core).start()
@@ -666,6 +715,9 @@
 
     for j in range(PARTS):
         final_copy(j, core).wait_send()
+    for j in range(PARTS):
+        for one in z_spread(0, spec, j) + [z_send(j, zz) for zz in far_z] + z_spread(2, out_mine, j):
+            one.wait_send()
     for group in (scatter, gather, add_sums, deliver):
         for one in group:
             one.drain()
@@ -787,12 +839,11 @@
             V((GROUPS, 2, 8, G), f32), V((GROUPS, 8, G), f32),
             V((GROUPS,) + two + (8, G), f32),
             V((GROUPS, B, G // GROUPS), f32), V((GROUPS, B // 2, G // GROUPS), f32), V((B // 2, 2 * B), f32),
-            V(two + (16, 2 * B), f32), V((2, 2, 2, 16, 2 * B), f32), V((2, 2, 16, 2 * B), f32), V((2, 16, 2 * B), f32),
-            V((16, 2 * B), f32),
-            DMA((4,)), DMA((4,)), DMA((PARTS, 3)), DMA((PARTS, 3)), DMA((PARTS, 4)), DMA((PARTS, 4)),
+            V(two + (16, 2 * B), f32), V((2, 2, 2, 16, 2 * B), f32), V((2, 2, 16, 2 * B), f32), V((4, 16, 2 * B), f32),
+            DMA((4,)), DMA((4,)), DMA((PARTS, 3)), DMA((PARTS, 3)), DMA((PARTS, 2)), DMA((PARTS, 2)),
             DMA((4,)), DMA((4,))] + [DMA((GROUPS, len(STRIPS), 4))] * 4 + [
-            DMA((GROUPS,)), DMA((GROUPS,)), DMA((PARTS, 4)), DMA((PARTS, 4)), DMA((PARTS, 4)), DMA((PARTS, 4)),
-            DMA((PARTS,)), DMA((PARTS,)), DMA((3,)), DMA((3,)),
+            DMA((GROUPS,)), DMA((GROUPS,)), DMA((PARTS, 2)), DMA((PARTS, 2)), DMA((PARTS, 2)), DMA((PARTS, 2)),
+            DMA((PARTS,)), DMA((PARTS,)), DMA((3,)), DMA((3,)), DMA((3, PARTS, 4)), DMA((3, PARTS, 4)),
         ],
         1, (mask, kernels, target) + blocks + consts, 59,
     )

time: 164 us -> 162 us (0.988)
  Pallas kernels: 161 us -> 159 us
where the time goes in v4:
time: 162 us
  Pallas kernels  159 us (98%)
  local copies, waits for them, and re-layouts  2.38 us (1%)
    pallas_call x1, Pallas kernels, call(): pl.pallas_call(kernel, out_shape=outs, in_specs=specs, out_specs=jax.tree...  145 us
    pallas_call x1, Pallas kernels, fast(): pl.pallas_call(final_kernel, out_shape=jax.ShapeDtypeStruct((R, N), f32),...  14.3 us

profile of v4, /device:TPU:1, one launch (start us, length us, event | category | flops | bytes accessed | tf_op | source)
XLA Modules:
  0.0 162.1 jit_solution(4297410065067194313)
XLA Ops:
  0.6 144.8 %shard_map.122 = (f32[2,2,2,2,2,16,1024]{6,5,4,3,2,1,0:T(8,128)}, f32[128,1024]{1,0:T(8,128)}) custom-call(bf16[512,4096]{1,0:T(8,128)(2,1)} %mask_hbm.1, f32[2,4,64,512]{3,2,1,0:T(8,128)} %kern_mine.1, s32[128,1024]{1,0:T(8,128)} %target_hbm.1, bf16[4,256,4096]{2,1,0:T(8,128)(2,1)} %constant.16.clone.bh_hbm, bf16[4,256,4096]{2,1,0:T(8,128)(2,1)} %constant.17.clone.bl_hbm, ...), custom_call_target="tpu_custom_call" | custom-call | tf_op jit(solution)/shard_map/pallas_call | solution.py:745
  145.4 0.0 copy-start
  145.4 1.6 copy-done
  147.0 0.0 copy-start.1
  147.0 14.3 %shard_map.123 = f32[512,4096]{1,0:T(8,128)} custom-call(f32[512,1024]{1,0:T(8,128)S(1)} %bitcast.1, bf16[4,256,4096]{2,1,0:T(8,128)(2,1)} %constant.16.clone.bh_hbm, bf16[4,256,4096]{2,1,0:T(8,128)(2,1)} %constant.17.clone.bl_hbm, bf16[2,512,2048]{2,1,0:T(8,128)(2,1)} %constant.18.clone.eh_hbm, bf16[2,512,2048]{2,1,0:T(8,128)(2,1)} %constant.19.clone.el_hbm), custom_call_target="tpu_custom_call" | custom-call | tf_op jit(solution)/shard_map/pallas_call | solution.py:850
  161.3 0.0 copy-done.1
  161.3 0.8 copy.14
Async XLA Ops:
  145.4 1.6 copy-start
  147.0 14.3 %copy-start.1 = (f32[128,1024]{1,0:T(8,128)S(1)}, f32[128,1024]{1,0:T(8,128)}, u32[]{:S(2)}) copy-start(f32[128,1024]{1,0:T(8,128)} %get-tuple-element.9) | copy-start | bytes 1572868

commit v5 on v4

--- a/solution.py
+++ b/solution.py
@@ -755,7 +755,8 @@
 
 
 def final_kernel(
-    total_ref, bh_hbm, bl_hbm, eh_hbm, el_hbm, out_hbm, slabh, slabl, eh, el, split, dh, dl, stage, slab_sem, table_sem, out_sem
+    total_hbm, bh_hbm, bl_hbm, eh_hbm, el_hbm, out_hbm,
+    total_ref, slabh, slabl, eh, el, split, dh, dl, stage, slab_sem, table_sem, out_sem,
 ):
     R, W, H = N // 8, 256, N // 2
     sp = lax.axis_index("space")
@@ -767,8 +768,10 @@
     tables = [
         pltpu.make_async_copy(src, dst, table_sem.at[i]) for i, (src, dst) in enumerate(((eh_hbm, eh), (el_hbm, el)))
     ]
-    for t in slabs:
+    arrive = pltpu.make_async_copy(total_hbm, total_ref, slab_sem.at[2])
+    for t in [arrive] + slabs:
         t.start()
+    arrive.wait()
     for i in range(2 * B // BLOCK):
         split[i] = total_ref[:, pl.ds(i * BLOCK, BLOCK)] * (1.0 / N)
     for t in slabs:
@@ -850,12 +853,12 @@
     gradient = pl.pallas_call(
         final_kernel,
         out_shape=jax.ShapeDtypeStruct((R, N), f32),
-        in_specs=[pl.BlockSpec(memory_space=pltpu.VMEM)] + [any_] * 4,
+        in_specs=[any_] * 5,
         out_specs=any_,
-        scratch_shapes=slab + [V(t.shape, bf16) for t in parity] + [
-            V((2 * groups, B, BLOCK), f32), V((2, R, B), bf16), V((2, R, B), bf16), V((2, 2, R, 256), f32), DMA((2,)), DMA((2,)), DMA((2, 2)),
+        scratch_shapes=[V((B, 2 * B), f32)] + slab + [V(t.shape, bf16) for t in parity] + [
+            V((2 * groups, B, BLOCK), f32), V((2, R, B), bf16), V((2, R, B), bf16), V((2, 2, R, 256), f32), DMA((3,)), DMA((2,)), DMA((2, 2)),
         ],
-        compiler_params=pltpu.CompilerParams(vmem_limit_bytes=48 * 2**20),
+        compiler_params=pltpu.CompilerParams(vmem_limit_bytes=59 * 2**20),
     )(total.reshape(B, 2 * B), *blocks, *parity)
     return gradient, resist
 

time: 162 us -> 161 us (level)
  no operation moved by 1% of the time
where the time goes in v5:
time: 161 us
  Pallas kernels  160 us (99%)
    pallas_call x1, Pallas kernels, call(): pl.pallas_call(kernel, out_shape=outs, in_specs=specs, out_specs=jax.tree...  145 us
    pallas_call x1, Pallas kernels, fast(): pl.pallas_call(final_kernel, out_shape=jax.ShapeDtypeStruct((R, N), f32),...  14.9 us

profile of v5, /device:TPU:1, one launch (start us, length us, event | category | flops | bytes accessed | tf_op | source)
XLA Modules:
  0.0 161.1 jit_solution(8049044194396101807)
XLA Ops:
  0.6 144.8 %shard_map.122 = (f32[2,2,2,2,2,16,1024]{6,5,4,3,2,1,0:T(8,128)}, f32[128,1024]{1,0:T(8,128)}) custom-call(bf16[512,4096]{1,0:T(8,128)(2,1)} %mask_hbm.1, f32[2,4,64,512]{3,2,1,0:T(8,128)} %kern_mine.1, s32[128,1024]{1,0:T(8,128)} %target_hbm.1, bf16[4,256,4096]{2,1,0:T(8,128)(2,1)} %constant.16.clone.bh_hbm, bf16[4,256,4096]{2,1,0:T(8,128)(2,1)} %constant.17.clone.bl_hbm, ...), custom_call_target="tpu_custom_call" | custom-call | tf_op jit(solution)/shard_map/pallas_call | solution.py:745
  145.4 0.0 copy-start
  145.5 14.9 %shard_map.123 = f32[512,4096]{1,0:T(8,128)} custom-call(f32[512,1024]{1,0:T(8,128)} %bitcast.1, bf16[4,256,4096]{2,1,0:T(8,128)(2,1)} %constant.16.clone.bh_hbm, bf16[4,256,4096]{2,1,0:T(8,128)(2,1)} %constant.17.clone.bl_hbm, bf16[2,512,2048]{2,1,0:T(8,128)(2,1)} %constant.18.clone.eh_hbm, bf16[2,512,2048]{2,1,0:T(8,128)(2,1)} %constant.19.clone.el_hbm), custom_call_target="tpu_custom_call" | custom-call | tf_op jit(solution)/shard_map/pallas_call | solution.py:853
  160.3 0.0 copy-done
  160.3 0.8 copy.14
Async XLA Ops:
  145.4 14.9 %copy-start = (f32[128,1024]{1,0:T(8,128)S(1)}, f32[128,1024]{1,0:T(8,128)}, u32[]{:S(2)}) copy-start(f32[128,1024]{1,0:T(8,128)} %get-tuple-element.9) | copy-start | bytes 1572868
